TPU v7x, 32 devices: a whole 2x2x4 slice. The times are simulated.
32 devices in a mesh: gz: 8 (over y, x, core), ma: 4 (over z).
Axes of the slice: x: 2, y: 2, z: 4, core: 2. Of those that a mesh axis runs over, the one named last changes fastest.
Arguments:
- bricks: bfloat16 [4096, 2048], P(('gz', 'ma')), may hold values from -7 to 7
- owners: int32 [4096, 1], P(('gz', 'ma')), may hold values from 0 to 31; in each aligned block of 128 rows (0 to 127, 128 to 255, ...) at most 8 rows name the same one
- tile_ids: int32 [4096], P(('gz', 'ma')), may hold values from 0 to 511
- counts: int32 [32], P(('gz', 'ma')), may hold values from 64 to 128, as said below
Outputs:
- brick_potential: bfloat16 [4096, 2048], P(('gz', 'ma'))
Inputs may be any that keep to these rules, and one draw needn't show every extreme that they name: `owners`: in the rows of one atom domain no device is named by more than 8 rows, and in every draw some device is named by exactly 8 rows of some domain. `counts`: some atom domain uses all 128 of its bricks.
All inputs are finite; a program needn't handle non-finite values.
Results may differ from a plain program's by a relative error of at most 0.0013.
Values may be sent and summed in bfloat16 or wider, within the bound.
No kernel may reach another device: no remote copies, remote signals or barrier semaphores. Data moves between devices by JAX's collectives and lax.ppermute only.
A program may use at most 192 MiB of HBM per device.

v0:
```python
import math

import jax
import jax.numpy as jnp
import ml_dtypes
import numpy as np
from jax import lax
from jax.experimental import pallas as pl
from jax.experimental.pallas import tpu as pltpu
from jax.sharding import PartitionSpec as P

NX = 512
NY = 512
SCREEN = 16
BZ = 4
BX = 8
BY = 64
CZ = 16


def hartley(length):
    indices = jnp.arange(length, dtype=jnp.int32)
    products = indices[:, None] * indices[None, :] % length
    angles = 2.0 * math.pi / length * products.astype(jnp.float32)
    return (jnp.cos(angles) + jnp.sin(angles)) / math.sqrt(length)


def second_difference(length, indices):
    return 2.0 - 2.0 * jnp.cos(2.0 * math.pi / length * indices.astype(jnp.float32))


def thomas(right_side, diagonal):
    start_zero = jnp.zeros(right_side.shape[1:], jnp.float32)

    def down(state_pair, plane):
        factor = 1.0 / (diagonal - state_pair[0])
        partial_value = (plane + state_pair[1]) * factor
        return ((factor, partial_value), (factor, partial_value))

    _, (factors, partials) = lax.scan(down, (start_zero, start_zero), right_side)

    def upward(beyond, factor_partial):
        solved = factor_partial[1] + factor_partial[0] * beyond
        return (solved, solved)

    _, solutions = lax.scan(upward, start_zero, (factors, partials), reverse=True)
    return solutions


def regroup(values):
    return lax.all_to_all(values, "ma", split_axis=2, concat_axis=1, tiled=True)


def on_device(bricks, owners, tile_ids, counts):
    domains = lax.axis_size(("gz", "ma"))
    group_count = lax.axis_size("ma")
    slab_count = lax.axis_size("gz")
    brick_rows, brick_cells = bricks.shape
    slot_count = max(2, 2 * brick_rows // domains)
    local_x = NX // group_count
    local_y = NY // group_count
    tiles_dev = CZ // BZ * (local_x // BX) * (NY // BY)
    highest = lax.Precision.HIGHEST
    target = owners[:, 0]
    row_order = jnp.arange(brick_rows, dtype=jnp.int32)
    earlier_same = (target[:, None] == target[None, :]) & (row_order[None, :] < row_order[:, None])
    within = jnp.sum(earlier_same.astype(jnp.int32), axis=1)
    slot_of = target * slot_count + within
    is_live = row_order < counts[0]
    loaded = jnp.where(is_live[:, None], bricks, jnp.zeros_like(bricks))
    outgoing = jnp.zeros((domains * slot_count, brick_cells), jnp.bfloat16).at[slot_of].set(loaded)
    out_ids = jnp.full((domains * slot_count,), tiles_dev, jnp.int32).at[slot_of].set(tile_ids)
    incoming, in_ids = (
        lax.all_to_all(outgoing, ("gz", "ma"), split_axis=0, concat_axis=0, tiled=True),
        lax.all_to_all(out_ids, ("gz", "ma"), split_axis=0, concat_axis=0, tiled=True),
    )
    picker = (jnp.arange(tiles_dev, dtype=jnp.int32)[:, None] == in_ids[None, :]).astype(
        jnp.bfloat16
    )
    deposit = jnp.dot(picker, incoming, preferred_element_type=jnp.float32)
    charge = deposit.reshape(CZ // BZ, local_x // BX, NY // BY, BZ, BX, BY)
    charge = charge.transpose(0, 3, 1, 4, 2, 5).reshape(CZ, local_x, NY)
    table_x = hartley(NX)
    table_y = hartley(NY)
    along_y = jnp.einsum("zxy,ky->zxk", charge, table_y, precision=highest)
    gathered_x = regroup(along_y)
    spectrum = jnp.einsum("zxk,jx->zjk", gathered_x, table_x, precision=highest)
    columns = lax.axis_index("ma") * local_y + jnp.arange(local_y, dtype=jnp.int32)
    lam_y = second_difference(NY, columns)
    screening = 1.0 / (SCREEN * SCREEN)
    slab_index = lax.axis_index("gz")
    lam_x = second_difference(NX, jnp.arange(NX, dtype=jnp.int32))
    diagonal = 2.0 + screening + lam_x[:, None] + lam_y[None, :]
    interior = spectrum[1:]
    particular = thomas(interior, diagonal)
    unit_rhs = jnp.zeros_like(interior).at[0].set(1.0)
    spike = thomas(unit_rhs, diagonal)
    near_weight = spike[0]
    far_weight = spike[-1]
    head_term = spectrum[0] + particular[0]
    tail_term = particular[-1]
    reduced_first = diagonal - near_weight
    reduced_rest = diagonal - 2.0 * near_weight
    start_zero = jnp.zeros_like(diagonal)
    heads, tails = (
        lax.all_gather(head_term[None], "gz", axis=0, tiled=True),
        lax.all_gather(tail_term[None], "gz", axis=0, tiled=True),
    )
    before = jnp.concatenate([start_zero[None], tails[:-1]], axis=0)
    sources = heads + before

    def chain_down(state_pair, packed):
        source, position = packed
        base_term = jnp.where(position == 0, reduced_first, reduced_rest)
        pivot_now = 1.0 / (base_term - far_weight * far_weight * state_pair[0])
        forward_part = pivot_now * (source + far_weight * state_pair[1])
        return ((pivot_now, forward_part), (pivot_now, forward_part))

    _, (pivots, forwards) = lax.scan(
        chain_down, (start_zero, start_zero), (sources, jnp.arange(slab_count, dtype=jnp.int32))
    )

    def chain_up(beyond, packed):
        plane_value = packed[1] + far_weight * packed[0] * beyond
        return (plane_value, plane_value)

    _, separators = lax.scan(chain_up, start_zero, (pivots, forwards), reverse=True)
    padded_sep = jnp.concatenate([separators, start_zero[None]], axis=0)
    own_plane = lax.dynamic_index_in_dim(padded_sep, slab_index, 0, keepdims=False)
    next_plane = lax.dynamic_index_in_dim(padded_sep, slab_index + 1, 0, keepdims=False)
    interior_sol = particular + own_plane[None] * spike + next_plane[None] * spike[::-1]
    modal = jnp.concatenate([own_plane[None], interior_sol], axis=0)
    back_x = jnp.einsum("zjk,jx->zkx", modal, table_x, precision=highest)
    gathered_y = regroup(back_x)
    potential = jnp.einsum("zkx,ky->zxy", gathered_y, table_y, precision=highest)
    pot_tiles = potential.reshape(CZ // BZ, BZ, local_x // BX, BX, NY // BY, BY)
    pot_tiles = (
        pot_tiles.transpose(0, 2, 4, 1, 3, 5).reshape(tiles_dev, brick_cells).astype(jnp.bfloat16)
    )
    padded_tiles = jnp.concatenate([pot_tiles, jnp.zeros((1, brick_cells), jnp.bfloat16)], axis=0)
    replies = padded_tiles[in_ids]
    returned = lax.all_to_all(replies, ("gz", "ma"), split_axis=0, concat_axis=0, tiled=True)
    result = returned[slot_of]
    return jnp.where(is_live[:, None], result, jnp.zeros_like(result))


DOMAINS = 32
GROUPS = 4
SLABS = 8
SEND = (4, 2, 5, 3, 0, 1, 6, 7)
ARRIVAL = (0, 4, 2, 5, 3, 1, 6, 7)
PARTS = 2
PART_PLANES = 2
TAKE_FIRST = (0, 4, 2, 5, 3, 1)
TAKE_LATER = (6, 7)
PAIR_SLOTS = 8
SLOTS = DOMAINS * PAIR_SLOTS
TILES = 512
BRICK_ROWS = 16
CELLS = 2048
LANES = 128
HALF = 64
SPOTS = 64
ROWS = BRICK_ROWS * SPOTS
PART_ROWS = ROWS // PARTS
PART_CELLS = CELLS // PARTS
DOT_ROWS = 512
PAIRS = 4
CLASSES = (0, 4, 1, 7, 2, 6, 3, 5)
HEAD_ROWS = 8
STEPS = 64
PLANES = 128
FULL = 32700.0
LOG_UNIT = 128.0
VMEM_BYTES = 24 * 1024 * 1024
ALL_VMEM_BYTES = 60 * 1024 * 1024


def split_table(table):
    high = table.astype(ml_dtypes.bfloat16)
    low = (table - high.astype(np.float64)).astype(ml_dtypes.bfloat16)
    return high, low


def line_tables():
    iy, k2 = np.arange(HALF)[:, None], np.arange(HALF)[None, :]
    tables = []
    for pair in range(PAIRS):
        table = np.zeros((LANES, LANES))
        for one in range(2):
            angle = 2.0 * np.pi / NY * (iy * (CLASSES[2 * pair + one] + 8 * k2) % NY)
            cosine, sine = np.cos(angle) / np.sqrt(NY), np.sin(angle) / np.sqrt(NY)
            there = slice(one * HALF, (one + 1) * HALF)
            if pair == 0:
                table[there, there] = cosine + sine
            else:
                table[:HALF, there] = cosine + sine
                table[HALF:, there] = (cosine - sine) * (1 - 2 * one)
        tables.append(table)

    def stacked(table):
        high, low = split_table(table)
        return np.concatenate(
            [np.concatenate([high, low], axis=1), np.concatenate([high, np.zeros_like(low)], axis=1)], axis=0
        )

    return np.stack([stacked(table) for table in tables]), np.stack([stacked(table.T) for table in tables])


def class_weights():
    pair, ty = np.arange(PAIRS)[:, None], np.arange(4)[None, :]
    cosine, sine = np.cos(np.pi / 4.0 * pair * ty), np.sin(np.pi / 4.0 * pair * ty)
    sine[0] = (-1.0) ** np.arange(4)
    sign = (-1.0) ** pair * np.ones((1, 4))
    return np.concatenate([cosine, sine, sign], axis=1).astype(np.float32)


def plane_tables(offsets, planes, turned):
    index = np.arange(PLANES)
    table = np.sqrt(2.0 / (PLANES + 1)) * np.sin(
        np.pi / (PLANES + 1) * ((index[:, None] + 1) * (index[None, :] + 1) % (2 * PLANES + 2))
    )
    each = []
    for own in range(SLABS):
        slabs = np.array([own ^ offset for offset in offsets])
        plane, tz = np.array(planes)[:, None, None], np.arange(BZ)[None, :, None]
        part = table[:, (slabs * CZ + tz * BZ + plane).reshape(-1)]
        high, low = split_table(part.T if turned else part)
        if turned or 3 * high.shape[1] <= 2 * LANES:
            each.append(np.concatenate([high, high, low], axis=1))
            continue
        top = np.concatenate([high, high], axis=1)
        bottom = np.concatenate([low, np.zeros_like(low)], axis=1)
        each.append(np.concatenate([top, bottom], axis=0))
    return np.stack(each)


def mode_tables():
    mu = 2.0 - 2.0 * np.cos(np.pi / (PLANES + 1) * (np.arange(PLANES) + 1))
    base = np.broadcast_to((mu + 1.0 / (SCREEN * SCREEN))[:, None], (PLANES, LANES))
    lam = 2.0 - 2.0 * np.cos(2.0 * np.pi / NY * np.arange(NY))
    lam = np.stack([lam[number::8] for number in CLASSES])
    return base.astype(np.float32), np.concatenate([lam, lam], axis=1).astype(np.float32)


def low_half(shape):
    return lax.broadcasted_iota(jnp.int32, shape, len(shape) - 1) < HALF


def split(values):
    high = values.astype(jnp.bfloat16)
    return high, (values - high.astype(jnp.float32)).astype(jnp.bfloat16)


def dot(left, right):
    return jnp.dot(left, right, preferred_element_type=jnp.float32)


def start_copies(pairs, sems):
    copies = [pltpu.make_async_copy(source, place, sems.at[at]) for at, (source, place) in enumerate(pairs)]
    for each in copies:
        each.start()
    return copies


def even_odd(first, second, low):
    crossed = pltpu.roll(jnp.where(low, second, first), HALF, 1)
    return jnp.where(low, first, crossed), jnp.where(low, crossed, second)


def write_left(at, here, lines, left_ref):
    rows = left_ref.shape[1] // 2
    for line, values in enumerate(lines):
        high, rest = split(values)
        there = slice(line * rows + here.start, line * rows + here.stop)
        left_ref[at, there, :LANES] = high
        left_ref[at, there, LANES:] = rest


def line_product(at, here, left_ref, table):
    products = []
    rows = left_ref.shape[1] // 2
    for line in range(2):
        there = slice(line * rows + here.start, line * rows + here.stop)
        both = dot(left_ref[at, there, :], table)
        products.append(both[:, :LANES] + both[:, LANES:])
    return even_odd(*products, low_half(products[0].shape))


def class_sums(points):
    half = [points[ty] + points[ty + 4] for ty in range(4)]
    rest = [points[ty] - points[ty + 4] for ty in range(4)]
    even, odd = half[0] + half[2], half[1] + half[3]
    turn = math.sqrt(0.5)
    across, along = turn * (rest[1] - rest[3]), turn * (rest[1] + rest[3])
    return (
        (even + odd, even - odd),
        (rest[0] + across, rest[2] + along),
        (half[0] - half[2], half[1] - half[3]),
        (rest[0] - across, along - rest[2]),
    )


def level_of(most):
    return jnp.floor(jnp.log2(jnp.maximum(most, 1e-30)) * LOG_UNIT) + 2.0


def inverse_of(level):
    return FULL * jnp.exp2(level * (-1.0 / LOG_UNIT))


def fixed_of(values):
    return jnp.floor(values + 0.5).astype(jnp.int32).astype(jnp.int16)


def head_of(level):
    return jnp.broadcast_to(level, (HEAD_ROWS, LANES)).astype(jnp.int32).astype(jnp.int16)


def unit_of(sent_ref):
    head = sent_ref[sent_ref.shape[0] - HEAD_ROWS :, :].astype(jnp.int32).astype(jnp.float32)
    return jnp.exp2(head[0:1] * (1.0 / LOG_UNIT)) * (1.0 / FULL)


def wide(sent_ref):
    block = sent_ref[: sent_ref.shape[0] - HEAD_ROWS, :]
    return block.astype(jnp.int32).astype(jnp.float32) * unit_of(sent_ref)


def turned_up(row):
    return jnp.broadcast_to(row, (row.shape[1], row.shape[1])).T


def pack_kernel(
    owner_in, tile_in, count_in, brick_in, out_ref, one_hot_ref,
    owner_ref, tile_ref, count_ref, brick_ref, ready_ref, sems, out_sems,
):
    cells = brick_in.at[:, pl.ds(0, PART_CELLS)]
    copies = start_copies(((owner_in, owner_ref), (tile_in, tile_ref), (count_in, count_ref), (cells, brick_ref)), sems)
    for each in copies[:3]:
        each.wait()
    owner, tile = owner_ref[...], tile_ref[...]
    brick_rows = owner.shape[1]
    square = (brick_rows, brick_rows)
    position = (tile & 7) * SPOTS + ((tile >> 3) & 15) * 4 + (tile >> 7)
    spot = (position + 1).astype(jnp.float32)
    high = jnp.floor(spot * (1.0 / 32.0))
    heads = jnp.where(low_half(square), turned_up(high), turned_up(spot - 32.0 * high)).astype(jnp.bfloat16)
    named = owner.astype(jnp.float32)
    earlier = lax.broadcasted_iota(jnp.int32, square, 0) < lax.broadcasted_iota(jnp.int32, square, 1)
    same = jnp.where((turned_up(named) == named) & earlier, 1.0, 0.0)
    within = jnp.sum(same, axis=0, keepdims=True).astype(jnp.int32)
    live = lax.broadcasted_iota(jnp.int32, owner.shape, 1) < count_ref[0]
    slot = jnp.where(live, owner * PAIR_SLOTS + within, SLOTS)
    copies[3].wait()
    copies = []
    rows = 64
    for part in range(SLOTS // rows):
        here = slice(part * rows, (part + 1) * rows)
        index = lax.broadcasted_iota(jnp.int32, (rows, brick_rows), 0) + part * rows
        picks = jnp.where(index == slot, 1.0, 0.0).astype(jnp.bfloat16)
        one_hot_ref[here, :] = picks
        ready_ref[here, :PART_CELLS] = dot(picks, brick_ref[...]).astype(jnp.bfloat16)
        ready_ref[here, PART_CELLS:] = dot(picks, heads).astype(jnp.bfloat16)
        some = pl.ds(part * rows, rows)
        copies.append(pltpu.make_async_copy(ready_ref.at[some], out_ref.at[some], out_sems.at[part]))
        copies[-1].start()
    for each in copies:
        each.wait()


def pack_later_kernel(brick_in, one_hot_ref, out_ref, back_ref, brick_ref, sems):
    [copy] = start_copies(((brick_in.at[:, pl.ds(PART_CELLS, PART_CELLS)], brick_ref),), sems)
    for part in range(SLOTS // LANES):
        here = slice(part * LANES, (part + 1) * LANES)
        back_ref[:, here] = one_hot_ref[here, :].astype(jnp.float32).T.astype(jnp.bfloat16)
    copy.wait()
    out_ref[...] = dot(one_hot_ref[...], brick_ref[...]).astype(jnp.bfloat16)


def write_across(brick_ref, across_ref):
    for part in range(SLOTS // LANES):
        here = slice(part * LANES, (part + 1) * LANES)
        head = brick_ref[here, PART_CELLS:].astype(jnp.float32)
        turned = pltpu.roll(head, HALF, 1)
        low = low_half(head.shape)
        places = jnp.where(low, head, turned) * 32.0 + jnp.where(low, turned, head)
        row = places.T[0:1, :].astype(jnp.int32) - 1
        for block in range(TILES // LANES):
            there = slice(block * LANES, (block + 1) * LANES)
            tile = lax.broadcasted_iota(jnp.int32, (LANES, LANES), 0) + block * LANES
            across_ref[there, here] = jnp.where(tile == row, 1.0, 0.0).astype(jnp.bfloat16)


def write_picks(across_ref, picks_ref):
    for part in range(SLOTS // LANES):
        here = slice(part * LANES, (part + 1) * LANES)
        for block in range(TILES // LANES):
            there = slice(block * LANES, (block + 1) * LANES)
            picks_ref[here, there] = across_ref[there, here].astype(jnp.float32).T.astype(jnp.bfloat16)


def forward_lines(own_ref, brick_ref, across_ref, table_in, sent_refs, left_ref, lines_ref, table_ref, sems):
    [copy] = start_copies(((table_in, table_ref),), sems)
    low = low_half((SPOTS, LANES))
    for q in range(0, BRICK_ROWS // PARTS, 4):
        charge = dot(across_ref[...], brick_ref[:, q * LANES : (q + 4) * LANES])
        for one in range(4):
            there = slice(one * LANES, (one + 1) * LANES)
            here = slice((q + one) * SPOTS, (q + one + 1) * SPOTS)
            points = [charge[ty * SPOTS : (ty + 1) * SPOTS, there] for ty in range(8)]
            for pair, (cosines, sines) in enumerate(class_sums(points)):
                write_left(pair, here, even_odd(cosines, sines, low), left_ref)
    copy.wait()
    for pair in range(PAIRS):
        for one, values in enumerate(line_product(pair, slice(0, PART_ROWS), left_ref, table_ref[pair])):
            most = jnp.max(jnp.abs(values).reshape(PART_ROWS // 8, 8, LANES), axis=0)
            level = level_of(jnp.max(most, axis=0, keepdims=True))
            lines_ref[2 * pair + one, :PART_ROWS, :] = fixed_of(values * inverse_of(level))
            lines_ref[2 * pair + one, PART_ROWS:, :] = head_of(level)
    for offset, sent_ref in zip(SEND, sent_refs):
        sent_ref[...] = lines_ref[own_ref[0] ^ offset]


def forward_first_kernel(own_ref, brick_ref, table_in, *refs):
    sent_refs, across_ref = refs[: len(SEND)], refs[len(SEND)]
    write_across(brick_ref, across_ref)
    forward_lines(own_ref, brick_ref, across_ref, table_in, sent_refs, *refs[len(SEND) + 1 :])


def forward_later_kernel(own_ref, brick_ref, across_ref, table_in, *refs):
    sent_refs, picks_ref = refs[: len(SEND)], refs[len(SEND)]
    write_picks(across_ref, picks_ref)
    forward_lines(own_ref, brick_ref, across_ref, table_in, sent_refs, *refs[len(SEND) + 1 :])


def grid_rows(slabs, plane, xq, tx):
    start = ((plane * 4 + xq) * SPOTS + tx * 4) * slabs
    return pl.ds(pl.multiple_of(start, 4 * slabs), 4 * slabs)


def plane_product(plane_ref, lines):
    high, rest = split(lines)
    rows = plane_ref.shape[0]
    if plane_ref.shape[1] == 3 * high.shape[0]:
        return dot(plane_ref[...], jnp.concatenate([high, rest, high], axis=0))
    both = dot(plane_ref[...], jnp.concatenate([high, rest], axis=0))
    return both[: rows // 2] + both[rows // 2 :]


def add_sines(got_refs, plane_ref, grid_ref, finish, swapped=False):
    slabs = len(got_refs)
    for at, got_ref in enumerate(got_refs):
        grid_ref[pl.ds(at, PART_ROWS, stride=slabs), :] = wide(got_ref)

    def planes(tx, xq):
        return jnp.concatenate(
            [grid_ref[grid_rows(slabs, plane, xq, tx), :] for plane in range(PART_PLANES)], axis=0
        )

    def sines(tx, _):
        lines = [planes(tx, xq) for xq in range(4)]
        if swapped:
            lines += [pltpu.roll(line, HALF, 1) for line in lines]
        modes = plane_product(plane_ref, jnp.concatenate(lines, axis=1))
        parts = [modes[:, at * LANES : (at + 1) * LANES] for at in range(len(lines))]
        for xq in range(4):
            finish(tx * 4 + xq, *parts[xq::4])
        return 0

    lax.fori_loop(0, 16, sines, 0, unroll=8)


def down_first_kernel(own_ref, *refs):
    count = len(ARRIVAL)
    planes_ref, base_ref, lam_ref, modes_ref, root_ref, gain_ref, power_ref, grid_ref = refs[count:]
    excess = base_ref[...] + lam_ref[pl.ds(own_ref[0], 1), :]
    spread = jnp.sqrt(excess * (excess + 4.0))
    root_ref[...] = 2.0 / (2.0 + excess + spread)
    gain_ref[...] = 1.0 / spread
    for part in range(2):
        here = pl.ds(part * PLANES // 2, PLANES // 2)
        square = root_ref[here, :] * root_ref[here, :]

        def raised(step, power):
            power_ref[step, here, :] = power
            return power * square

        lax.fori_loop(0, STEPS, raised, jnp.ones(square.shape, jnp.float32), unroll=8)

    def finish(line, values):
        modes_ref[line] = values

    add_sines(refs[:count], planes_ref.at[own_ref[0]], grid_ref, finish)


def down_middle_kernel(own_ref, *refs):
    count = len(TAKE_FIRST)
    sums_ref, root_ref, planes_ref, out_ref, grid_ref = refs[count:]

    def finish(line, values):
        values = sums_ref[line] + values
        out_ref[line] = values + root_ref[...] * pltpu.roll(values, HALF, 1)

    add_sines(refs[:count], planes_ref.at[own_ref[0]], grid_ref, finish)


def down_later_kernel(own_ref, *refs):
    count = len(TAKE_LATER)
    sums_ref, root_ref, planes_ref, walk_ref, end_ref, grid_ref, modes_ref, last_ref = refs[count:]

    def finish(line, values, swapped):
        modes_ref[line] = sums_ref[line] + (values + root_ref[...] * swapped)

    add_sines(refs[:count], planes_ref.at[own_ref[0]], grid_ref, finish, True)
    part_rows = 64
    low = low_half((part_rows, LANES))
    for part in range(PLANES // part_rows):
        here = pl.ds(part * part_rows, part_rows)
        square = root_ref[here, :] * root_ref[here, :]

        def walk(step, held):
            held = square * held + jnp.where(low, modes_ref[STEPS - 1 - step, here, :], modes_ref[step, here, :])
            walk_ref[step, here, :] = held
            return held

        last_ref[here, :] = lax.fori_loop(0, STEPS, walk, jnp.zeros((part_rows, LANES), jnp.float32), unroll=8)
    last = last_ref[...]
    level = level_of(jnp.max(jnp.abs(last), axis=0, keepdims=True))
    end_ref[:PLANES, :] = fixed_of(last * inverse_of(level))
    end_ref[PLANES:, :] = head_of(level)


def local_kernel(walk_ref, root_ref, gain_ref, local_ref):
    part_rows = 64
    low = low_half((part_rows, LANES))
    for part in range(PLANES // part_rows):
        here = pl.ds(part * part_rows, part_rows)
        root, gain = root_ref[here, :], gain_ref[here, :]
        zero = jnp.zeros(root.shape, jnp.float32)

        def line(step, ahead_before, behind_after):
            near = jnp.where(low, walk_ref[STEPS - 1 - step, here, :], walk_ref[step, here, :])
            far = pltpu.roll(jnp.where(low, behind_after, ahead_before), HALF, 1)
            local_ref[step, here, :] = gain * (near + root * far)

        def inner(step, _):
            line(step, walk_ref[step - 1, here, :], walk_ref[STEPS - 2 - step, here, :])
            return 0

        line(0, zero, walk_ref[STEPS - 2, here, :])
        lax.fori_loop(1, STEPS - 1, inner, 0, unroll=6)
        line(STEPS - 1, walk_ref[STEPS - 2, here, :], zero)


def up_kernel(own_ref, local_ref, power_ref, root_ref, gain_ref, *refs):
    end_refs, plane_ref = refs[:GROUPS], refs[GROUPS].at[own_ref[0]]
    count = GROUPS + 1 + len(SEND)
    sent_refs = refs[GROUPS + 1 : count]
    rise_ref, fall_ref, grid_ref, level_ref = refs[count:]
    low = low_half((PLANES, LANES))
    root = root_ref[...]
    square = root * root
    across = square
    for _ in range(6):
        across = across * across
    around = across
    for _ in range(2):
        around = around * around
    ends = [wide(end_ref) for end_ref in end_refs]
    entering = jnp.zeros((PLANES, LANES), jnp.float32)
    for step in range(GROUPS - 1, -1, -1):
        entering = entering * across + jnp.where(low, ends[GROUPS - 1 - step], ends[(step + 1) % GROUPS])
    entering = gain_ref[...] * entering / (1.0 - around)
    straight, turned = square * entering, root * pltpu.roll(entering, HALF, 1)
    rise_ref[...] = jnp.where(low, turned, straight)
    fall_ref[...] = jnp.where(low, straight, turned)
    slabs = len(sent_refs)

    def solved(step):
        reach = rise_ref[...] * power_ref[step] + fall_ref[...] * power_ref[STEPS - 1 - step]
        return local_ref[step] + reach

    def sines(tx, most):
        lines = plane_product(plane_ref, jnp.concatenate([solved(tx * 4 + xq) for xq in range(4)], axis=1))
        for xq in range(4):
            part = lines[:, xq * LANES : (xq + 1) * LANES]
            most = jnp.maximum(most, jnp.max(jnp.abs(part).reshape(4 * BZ, slabs, LANES), axis=0))
            for plane in range(BZ):
                grid_ref[grid_rows(slabs, plane, xq, tx), :] = part[plane * 4 * slabs : (plane + 1) * 4 * slabs]
        return most

    most = lax.fori_loop(0, 16, sines, jnp.zeros((slabs, LANES), jnp.float32), unroll=8)
    level_ref[...] = level_of(most)
    for at, sent_ref in enumerate(sent_refs):
        level = level_ref[at : at + 1, :]
        sent_ref[:ROWS, :] = fixed_of(grid_ref[pl.ds(at, ROWS, stride=slabs), :] * inverse_of(level))
        sent_ref[ROWS:, :] = head_of(level)


def take_lines(own_ref, offsets, got_refs, left_ref, lines_ref):
    own = own_ref[0]
    pairs = list(dict.fromkeys(offset // 2 for offset in offsets))
    for offset, got_ref in zip(offsets, got_refs):
        lines_ref[2 * pairs.index(offset // 2) + ((own ^ offset) & 1)] = wide(got_ref)
    low = low_half((DOT_ROWS, LANES))
    for at in range(len(pairs)):
        for start in range(0, ROWS, DOT_ROWS):
            here = slice(start, start + DOT_ROWS)
            write_left(at, here, even_odd(lines_ref[2 * at, here, :], lines_ref[2 * at + 1, here, :], low), left_ref)
    return [(own >> 1) ^ pair for pair in pairs]


def point_parts(pair, cosines, sines, weight_ref):
    for ty in range(4):
        part = weight_ref[pair, ty] * cosines + weight_ref[pair, 4 + ty] * sines
        yield ty, part
        yield ty + 4, weight_ref[pair, 8] * part


def reply_first_kernel(own_ref, weight_ref, *refs):
    count = len(TAKE_FIRST)
    table_ref, sums_ref, lines_ref, left_ref = refs[count:]
    pairs = take_lines(own_ref, TAKE_FIRST, refs[:count], left_ref, lines_ref)
    for at, pair in enumerate(pairs):
        for part in range(ROWS // DOT_ROWS):
            here = slice(part * DOT_ROWS, (part + 1) * DOT_ROWS)
            cosines, sines = line_product(at, here, left_ref, table_ref[pair])
            for ty, values in point_parts(pair, cosines, sines, weight_ref):
                sums_ref[ty, here, :] = values if at == 0 else sums_ref[ty, here, :] + values


def reply_later_kernel(own_ref, weight_ref, *refs):
    count = len(TAKE_LATER)
    sums_ref, picks_ref, table_ref, out_ref, lines_ref, left_ref, pot_ref = refs[count:]
    [pair] = take_lines(own_ref, TAKE_LATER, refs[:count], left_ref, lines_ref)
    for part in range(ROWS // DOT_ROWS):
        here = slice(part * DOT_ROWS, (part + 1) * DOT_ROWS)
        cosines, sines = line_product(0, here, left_ref, table_ref[pair])
        for ty, values in point_parts(pair, cosines, sines, weight_ref):
            values = (sums_ref[ty, here, :] + values).astype(jnp.bfloat16)
            for one in range(DOT_ROWS // SPOTS):
                q = part * (DOT_ROWS // SPOTS) + one
                pot_ref[ty * SPOTS : (ty + 1) * SPOTS, q * LANES : (q + 1) * LANES] = values[
                    one * SPOTS : (one + 1) * SPOTS
                ]
    for q in range(0, BRICK_ROWS, 4):
        there = slice(q * LANES, (q + 4) * LANES)
        out_ref[:, there] = dot(picks_ref[...], pot_ref[:, there]).astype(jnp.bfloat16)


def unpack_kernel(back_ref, got_ref, out_ref):
    for q in range(0, BRICK_ROWS, 4):
        there = slice(q * LANES, (q + 4) * LANES)
        out_ref[:, there] = dot(back_ref[...], got_ref[:, there]).astype(jnp.bfloat16)


def call(kernel, name, operands, spaces, outs, places, scratch, vmem=VMEM_BYTES):
    return pl.pallas_call(
        kernel,
        out_shape=outs,
        in_specs=[pl.BlockSpec(memory_space=space) for space in spaces],
        out_specs=[pl.BlockSpec(memory_space=space) for space in places],
        scratch_shapes=scratch,
        compiler_params=pltpu.CompilerParams(vmem_limit_bytes=vmem),
        name=name,
    )(*operands)


def on_device_8x4(bricks, owners, tile_ids, counts):
    V, S, H = pltpu.VMEM, pltpu.SMEM, pltpu.HBM
    f32, bf16, i32, i16 = jnp.float32, jnp.bfloat16, jnp.int32, jnp.int16
    shape, dma = jax.ShapeDtypeStruct, pltpu.SemaphoreType.DMA
    brick_rows = bricks.shape[0]
    lines_in, lines_out = (jnp.asarray(each) for each in line_tables())
    weights = jnp.asarray(class_weights())
    lines_in = pltpu.with_memory_space_constraint(lines_in, H)
    planes_in = [
        jnp.asarray(plane_tables(offsets, planes, False))
        for offsets, planes in ((ARRIVAL, (0, 1)), (TAKE_FIRST, (2, 3)), (TAKE_LATER, (2, 3)))
    ]
    planes_out = jnp.asarray(plane_tables(SEND, range(BZ), True))
    base, lam = (jnp.asarray(each) for each in mode_tables())
    own = lax.axis_index("gz").astype(i32).reshape(1)
    sent_shape = shape((ROWS + HEAD_ROWS, LANES), i16)
    end_shape = shape((PLANES + HEAD_ROWS, LANES), i16)
    cube, flat, sums_shape = (STEPS, PLANES, LANES), (PLANES, LANES), (8, ROWS, LANES)
    line, packed = (ROWS, LANES), [(SLOTS, PART_CELLS + LANES), (SLOTS, PART_CELLS)]
    part_shape = shape((PART_ROWS + HEAD_ROWS, LANES), i16)

    def all_ways(values):
        return lax.all_to_all(values, ("gz", "ma"), split_axis=0, concat_axis=0, tiled=True)

    def over_slabs(offset, values):
        return lax.ppermute(values, "gz", [(g, g ^ offset) for g in range(SLABS)]) if offset else values

    def round_groups(values, step):
        return lax.ppermute(values, "ma", [(m, (m + step) % GROUPS) for m in range(GROUPS)]) if step else values

    def exchanged(sent):
        sent = dict(zip(SEND, sent))
        return [over_slabs(offset, sent[offset]) for offset in ARRIVAL]

    outgoing, one_hot = call(
        pack_kernel,
        "pack",
        (owners.reshape(1, brick_rows), tile_ids.reshape(1, brick_rows), counts, bricks),
        [H] * 4,
        [shape(packed[0], bf16), shape((SLOTS, brick_rows), bf16)],
        [H, V],
        [
            V((1, brick_rows), i32),
            V((1, brick_rows), i32),
            S((1,), i32),
            V((brick_rows, PART_CELLS), bf16),
            V(packed[0], bf16),
            dma((4,)),
            dma((4,)),
        ],
        ALL_VMEM_BYTES,
    )
    outgoing_later, back = call(
        pack_later_kernel,
        "pack_later",
        (bricks, one_hot),
        [H, V],
        [shape(packed[1], bf16), shape((brick_rows, SLOTS), bf16)],
        [V, V],
        [V((brick_rows, PART_CELLS), bf16), dma((1,))],
    )
    incoming = [all_ways(outgoing), all_ways(outgoing_later)]
    forward_scratch = [
        V((PAIRS, 2 * PART_ROWS, 2 * LANES), bf16),
        V((len(SEND), *part_shape.shape), i16),
        V(lines_in.shape, bf16),
        dma((1,)),
    ]
    *sent, across = call(
        forward_first_kernel,
        "forward_first",
        (own, incoming[0], lines_in),
        [S, V, H],
        [part_shape] * len(SEND) + [shape((TILES, SLOTS), bf16)],
        [V] * (len(SEND) + 1),
        forward_scratch,
    )
    first = exchanged(sent)
    second, first[1], first[2] = lax.optimization_barrier((incoming[1], first[1], first[2]))
    *sent, picks = call(
        forward_later_kernel,
        "forward_later",
        (own, second, across, lines_in),
        [S, V, V, H],
        [part_shape] * len(SEND) + [shape((SLOTS, TILES), bf16)],
        [V] * (len(SEND) + 1),
        forward_scratch,
    )
    later = exchanged(sent)
    sums, root, gain, power = call(
        down_first_kernel,
        "down_first",
        (own, *first, planes_in[0], base, lam),
        [S] + [V] * (len(first) + 3),
        [shape(cube, f32), shape(flat, f32), shape(flat, f32), shape(cube, f32)],
        [V] * 4,
        [
            V((len(first) * PART_ROWS, LANES), f32),
        ],
    )
    middle, later = later[: len(TAKE_FIRST)], later[len(TAKE_FIRST) :]
    (sums,) = call(
        down_middle_kernel,
        "down_middle",
        (own, *middle, sums, root, planes_in[1]),
        [S] + [V] * (len(middle) + 3),
        [shape(cube, f32)],
        [V],
        [V((len(middle) * PART_ROWS, LANES), f32)],
    )
    walk, end = call(
        down_later_kernel,
        "down_later",
        (own, *later, sums, root, planes_in[2]),
        [S] + [V] * (len(later) + 3),
        [shape(cube, f32), end_shape],
        [V, V],
        [
            V((len(later) * PART_ROWS, LANES), f32),
            V(cube, f32),
            V(flat, f32),
        ],
    )
    ends = [round_groups(end, step) for step in range(GROUPS)]
    (local,) = call(local_kernel, "local", (walk, root, gain), [V] * 3, [shape(cube, f32)], [V], [])
    sent = call(
        up_kernel,
        "up",
        (own, local, power, root, gain, *ends, planes_out),
        [S] + [V] * (5 + GROUPS),
        [sent_shape] * len(SEND),
        [V] * len(SEND),
        [
            V(flat, f32),
            V(flat, f32),
            V((len(SEND) * ROWS, LANES), f32),
            V((len(SEND), LANES), f32),
        ],
    )
    got = exchanged(sent)
    first, later = got[: len(TAKE_FIRST)], got[len(TAKE_FIRST) :]
    (sums,) = call(
        reply_first_kernel,
        "reply_first",
        (own, weights, *first, lines_out),
        [S, S] + [V] * (len(first) + 1),
        [shape(sums_shape, f32)],
        [V],
        [V((len(first), *line), f32), V((len(first) // 2, 2 * ROWS, 2 * LANES), bf16)],
    )
    (replies,) = call(
        reply_later_kernel,
        "reply_later",
        (own, weights, *later, sums, picks, lines_out),
        [S, S] + [V] * (len(later) + 3),
        [shape((SLOTS, CELLS), bf16)],
        [V],
        [
            V((len(later), *line), f32),
            V((len(later) // 2, 2 * ROWS, 2 * LANES), bf16),
            V((TILES, CELLS), bf16),
        ],
    )
    (result,) = call(
        unpack_kernel,
        "unpack",
        (back, all_ways(replies)),
        [V, V],
        [shape((brick_rows, CELLS), bf16)],
        [V],
        [],
    )
    return result


def solution(mesh):
    in_specs = (P(("gz", "ma"), None), P(("gz", "ma"), None), P(("gz", "ma")), P(("gz", "ma")))
    out_specs = P(("gz", "ma"), None)
    body = on_device_8x4 if (mesh.shape["gz"], mesh.shape["ma"]) == (SLABS, GROUPS) else on_device
    return jax.shard_map(body, mesh=mesh, in_specs=in_specs, out_specs=out_specs, check_vma=False)
```

profile of v0, /device:TPU:1, one launch (start us, length us, event | category | flops | bytes accessed | tf_op | source)
XLA Modules:
  0.0 137.7 jit_solution(3335363728296035381)
XLA Ops:
  0.8 2.7 %pack.1 = (bf16[256,1152]{1,0:T(8,128)(2,1)}, bf16[256,128]{1,0:T(8,128)(2,1)}) custom-call(s32[1,128]{1,0:T(1,128)} %bitcast.14, s32[1,128]{1,0:T(1,128)} %bitcast.15, s32[1]{0:T(128)S(6)} %copy.14.count_in, bf16[128,2048]{1,0:T(8,128)(2,1)} %brick_in.3), custom_call_target="tpu_custom_call" | custom-call | tf_op jit(solution)/shard_map/pack/pallas_call | solution.py:659
  3.5 7.1 %all-to-all-start.1 = ((bf16[32,8,1152]{2,1,0:T(8,128)(2,1)}), bf16[32,8,1152]{2,1,0:T(8,128)(2,1)S(1)}, u32[]{:S(2)}, u32[]{:S(2)}) async-start(bf16[32,8,1152]{2,1,0:T(8,128)(2,1)} %bitcast.13), calls=%async_computation.1 | async-start | bytes 1179648 | tf_op jit(solution)/shard_map/all_to_all | solution.py:692
  13.7 13.6 %all-to-all-done.1 = bf16[32,8,1152]{2,1,0:T(8,128)(2,1)S(1)} async-done(((bf16[32,8,1152]{2,1,0:T(8,128)(2,1)}), bf16[32,8,1152]{2,1,0:T(8,128)(2,1)S(1)}, u32[]{:S(2)}, u32[]{:S(2)}) %all-to-all-start.1) | async-done | bytes 589856 | tf_op jit(solution)/shard_map/all_to_all | solution.py:692
  27.3 3.2 %all-to-all-start = ((bf16[32,8,1024]{2,1,0:T(8,128)(2,1)}), bf16[32,8,1024]{2,1,0:T(8,128)(2,1)S(1)}, u32[]{:S(2)}, u32[]{:S(2)}) async-start(bf16[32,8,1024]{2,1,0:T(8,128)(2,1)} %bitcast.3), calls=%async_computation | async-start | bytes 1048576 | tf_op jit(solution)/shard_map/all_to_all | solution.py:692
  30.4 3.7 %forward_first.1 = (s16[520,128]{1,0:T(8,128)(2,1)S(1)}, s16[520,128]{1,0:T(8,128)(2,1)S(1)}, s16[520,128]{1,0:T(8,128)(2,1)}, s16[520,128]{1,0:T(8,128)(2,1)}, ...) custom-call(s32[1]{0:T(128)} %bitcast.2.own_ref, ...), custom_call_target="tpu_custom_call" | custom-call | tf_op jit(solution)/shard_map/forward_first/pallas_call | solution.py:659
  38.2 2.7 %collective-permute-done.refs_1_ = s16[520,128]{1,0:T(8,128)(2,1)S(1)} collective-permute-done((s16[520,128]{1,0:T(8,128)(2,1)S(1)}, s16[520,128]{1,0:T(8,128)(2,1)S(1)}, u32[]{:S(2)}, u32[]{:S(2)}) %collective-permute-start) | collective-permute-done | bytes 133152 | tf_op jit(solution)/shard_map/ppermute | solution.py:695
  40.9 1.7 %collective-permute-start.12 = (s16[520,128]{1,0:T(8,128)(2,1)S(1)}, s16[520,128]{1,0:T(8,128)(2,1)S(1)}, u32[]{:S(2)}, u32[]{:S(2)}) collective-permute-start(s16[520,128]{1,0:T(8,128)(2,1)S(1)} %get-tuple-element.66), channel_id=1, source_target_pairs={{0,24},{4,28},{8,16},{12,20},{16,8},{20,12},{24,0},{28,4},{1,25},{... | collective-permute-start | bytes 399368 | tf_op jit(solution)/shard_map/ppermute | solution.py:695
  42.6 2.0 %collective-permute-start.13 = (s16[520,128]{1,0:T(8,128)(2,1)S(1)}, s16[520,128]{1,0:T(8,128)(2,1)S(1)}, u32[]{:S(2)}, u32[]{:S(2)}) collective-permute-start(s16[520,128]{1,0:T(8,128)(2,1)S(1)} %get-tuple-element.67), channel_id=1, source_target_pairs={{0,28},{4,24},{8,20},{12,16},{16,12},{20,8},{24,4},{28,0},{1,29},{... | collective-permute-start | bytes 399368 | tf_op jit(solution)/shard_map/ppermute | solution.py:695
  45.8 3.0 %forward_later.1 = (s16[520,128]{1,0:T(8,128)(2,1)S(1)}, s16[520,128]{1,0:T(8,128)(2,1)S(1)}, s16[520,128]{1,0:T(8,128)(2,1)S(1)}, s16[520,128]{1,0:T(8,128)(2,1...) custom-call(s32[1]{0:T(128)} %bitcast.2.own_ref, ...), custom_call_target="tpu_custom_call" | custom-call | tf_op jit(solution)/shard_map/forward_later/pallas_call | solution.py:659
  52.2 2.8 %collective-permute-done.4.refs_1_ = s16[520,128]{1,0:T(8,128)(2,1)S(1)} collective-permute-done((s16[520,128]{1,0:T(8,128)(2,1)S(1)}, s16[520,128]{1,0:T(8,128)(2,1)S(1)}, u32[]{:S(2)}, u32[]{:S(2)}) %collective-permute-start.4) | collective-permute-done | bytes 133152 | tf_op jit(solution)/shard_map/ppermute | solution.py:695
  57.8 1.8 %down_first.1 = (f32[64,128,128]{2,1,0:T(8,128)S(1)}, f32[128,128]{1,0:T(8,128)S(1)}, f32[128,128]{1,0:T(8,128)S(1)}, f32[64,128,128]{2,1,0:T(8,128)S(1)}) custom-call(s32[1]{0:T(128)} %bitcast.2.own_ref, s16[520,128]{1,0:T(8,128)(2,1)S(1)} %get-tuple-element.60.refs_0_, s16[520,128]{1,0:T(8,128)(2,1)S(1)} %collective-permute-done.refs_1_, ...), custom_call_target="tpu_custom_call" | custom-call | tf_op jit(solution)/shard_map/down_first/pallas_call | solution.py:659
  59.7 1.7 %down_middle.1.refs_2_ = f32[64,128,128]{2,1,0:T(8,128)S(1)} custom-call(s32[1]{0:T(128)} %bitcast.2.own_ref, s16[520,128]{1,0:T(8,128)(2,1)S(1)} %get-tuple-element.54.refs_0_, s16[520,128]{1,0:T(8,128)(2,1)S(1)} %collective-permute-done.4.refs_1_, s16[520,128]{1,0:T(8,128)(2,1)S(1)} %collective-permute-done.5.refs_2_, ...), custom_call_target="tpu_custom_call" | custom-call | tf_op jit(solution)/shard_map/down_middle/pallas_call | solution.py:659
  61.5 2.5 %collective-permute-done.3.refs_1_ = s16[520,128]{1,0:T(8,128)(2,1)S(1)} collective-permute-done((s16[520,128]{1,0:T(8,128)(2,1)S(1)}, s16[520,128]{1,0:T(8,128)(2,1)S(1)}, u32[]{:S(2)}, u32[]{:S(2)}) %collective-permute-start.3) | collective-permute-done | bytes 133152 | tf_op jit(solution)/shard_map/ppermute | solution.py:695
  63.9 2.1 %down_later.1 = (f32[64,128,128]{2,1,0:T(8,128)S(1)}, s16[136,128]{1,0:T(8,128)(2,1)S(1)}) custom-call(s32[1]{0:T(128)} %bitcast.2.own_ref, s16[520,128]{1,0:T(8,128)(2,1)S(1)} %collective-permute-done.2.refs_0_, s16[520,128]{1,0:T(8,128)(2,1)S(1)} %collective-permute-done.3.refs_1_, f32[64,128,128]{2,1,0:T(8,128)S(1)} %down_middle.1.refs_2_, ...), custom_call_target="tpu_custom_call" | custom-call | tf_op jit(solution)/shard_map/down_later/pallas_call | solution.py:659
  66.1 2.6 %collective-permute-start.16 = (s16[136,128]{1,0:T(8,128)(2,1)S(1)}, s16[136,128]{1,0:T(8,128)(2,1)S(1)}, u32[]{:S(2)}, u32[]{:S(2)}) collective-permute-start(s16[136,128]{1,0:T(8,128)(2,1)S(1)} %get-tuple-element.73.refs_0_), channel_id=1, source_target_pairs={{0,3},{1,0},{2,1},{3,2},{4,7},{5,4},{6,5},{7,6},{8,11},{9,8},{10,9... | collective-permute-start | bytes 104456 | tf_op jit(solution)/shard_map/ppermute | solution.py:698
  69.9 3.0 %local.1.local_ref = f32[64,128,128]{2,1,0:T(8,128)S(1)} custom-call(f32[64,128,128]{2,1,0:T(8,128)S(1)} %get-tuple-element.70.walk_ref, f32[128,128]{1,0:T(8,128)S(1)} %get-tuple-element.69.refs_7_.refs_3_.root_ref, f32[128,128]{1,0:T(8,128)S(1)} %get-tuple-element.71.gain_ref), custom_call_target="tpu_custom_call" | custom-call | tf_op jit(solution)/shard_map/local/pallas_call | solution.py:659
  73.4 4.5 %up.1 = (s16[1032,128]{1,0:T(8,128)(2,1)S(1)}, s16[1032,128]{1,0:T(8,128)(2,1)S(1)}, s16[1032,128]{1,0:T(8,128)(2,1)S(1)}, s16[1032,128]{1,0:T(8,128)(2,1)S(1)},...) custom-call(s32[1]{0:T(128)} %bitcast.2.own_ref, ...), custom_call_target="tpu_custom_call" | custom-call | tf_op jit(solution)/shard_map/up/pallas_call | solution.py:659
  79.6 2.7 %collective-permute-start.21 = (s16[1032,128]{1,0:T(8,128)(2,1)S(1)}, s16[1032,128]{1,0:T(8,128)(2,1)S(1)}, u32[]{:S(2)}, u32[]{:S(2)}) collective-permute-start(s16[1032,128]{1,0:T(8,128)(2,1)S(1)} %get-tuple-element.79), channel_id=1, source_target_pairs={{0,20},{4,16},{8,28},{12,24},{16,4},{20,0},{24,12},{28,8},{1,21},{... | collective-permute-start | bytes 792584 | tf_op jit(solution)/shard_map/ppermute | solution.py:695
  85.7 5.5 %collective-permute-start.18 = (s16[1032,128]{1,0:T(8,128)(2,1)S(1)}, s16[1032,128]{1,0:T(8,128)(2,1)S(1)}, u32[]{:S(2)}, u32[]{:S(2)}) collective-permute-start(s16[1032,128]{1,0:T(8,128)(2,1)S(1)} %get-tuple-element.75), channel_id=1, source_target_pairs={{0,28},{4,24},{8,20},{12,16},{16,12},{20,8},{24,4},{28,0},{1,29},{... | collective-permute-start | bytes 792584 | tf_op jit(solution)/shard_map/ppermute | solution.py:695
  92.7 2.3 %collective-permute-done.22.refs_4_ = s16[1032,128]{1,0:T(8,128)(2,1)S(1)} collective-permute-done((s16[1032,128]{1,0:T(8,128)(2,1)S(1)}, s16[1032,128]{1,0:T(8,128)(2,1)S(1)}, u32[]{:S(2)}, u32[]{:S(2)}) %collective-permute-start.22) | collective-permute-done | bytes 264224 | tf_op jit(solution)/shard_map/ppermute | solution.py:695
  95.0 4.4 %reply_first.1.refs_2_ = f32[8,1024,128]{2,1,0:T(8,128)S(1)} custom-call(s32[1]{0:T(128)} %bitcast.2.own_ref, f32[4,12]{1,0:T(4,128)S(1)} %copy-done.8, s16[1032,128]{1,0:T(8,128)(2,1)S(1)} %get-tuple-element.76.refs_0_, s16[1032,128]{1,0:T(8,128)(2,1)S(1)} %collective-permute-done.19.refs_1_, s16[1032,128]{1,0:T(8,128)(2,1)S(1)} %collective-permute-done.20.refs_2_, ...), custom_call_target="tpu_custom_call" | custom-call | tf_op jit(solution)/shard_map/reply_first/pallas_call | solution.py:659
  99.4 4.8 %collective-permute-done.18.refs_1_ = s16[1032,128]{1,0:T(8,128)(2,1)S(1)} collective-permute-done((s16[1032,128]{1,0:T(8,128)(2,1)S(1)}, s16[1032,128]{1,0:T(8,128)(2,1)S(1)}, u32[]{:S(2)}, u32[]{:S(2)}) %collective-permute-start.18) | collective-permute-done | bytes 264224 | tf_op jit(solution)/shard_map/ppermute | solution.py:695
  104.2 2.6 %reply_later.1 = bf16[256,2048]{1,0:T(8,128)(2,1)S(1)} custom-call(s32[1]{0:T(128)} %bitcast.2.own_ref, f32[4,12]{1,0:T(4,128)S(1)} %copy-done.8, s16[1032,128]{1,0:T(8,128)(2,1)S(1)} %collective-permute-done.17.refs_0_, s16[1032,128]{1,0:T(8,128)(2,1)S(1)} %collective-permute-done.18.refs_1_, f32[8,1024,128]{2,1,0:T(8,128)S(1)} %reply_first.1.refs_2_, ...), custom_call_target="tpu_custom_call" | custom-call | tf_op jit(solution)/shard_map/reply_later/pallas_call | solution.py:659
  106.8 29.7 %all_to_all.34 = bf16[32,8,2048]{2,1,0:T(8,128)(2,1)S(1)} all-to-all(bf16[32,8,2048]{2,1,0:T(8,128)(2,1)S(1)} %bitcast.10), channel_id=1, replica_groups=mesh['gz'=8,'ma'=4] {'gz','ma'}, dimensions={0} | all-to-all | bytes 2097152 | tf_op jit(solution)/shard_map/all_to_all | solution.py:692
  (61 shorter events, 24.2 us)
Async XLA Ops:
  3.5 23.8 %all-to-all-start.1 = ((bf16[32,8,1152]{2,1,0:T(8,128)(2,1)}), bf16[32,8,1152]{2,1,0:T(8,128)(2,1)S(1)}, u32[]{:S(2)}, u32[]{:S(2)}) async-start(bf16[32,8,1152]{2,1,0:T(8,128)(2,1)} %bitcast.13), calls=%async_computation.1 | async-start | bytes 1179648 | tf_op jit(solution)/shard_map/all_to_all | solution.py:692
  27.3 18.6 %all-to-all-start = ((bf16[32,8,1024]{2,1,0:T(8,128)(2,1)}), bf16[32,8,1024]{2,1,0:T(8,128)(2,1)S(1)}, u32[]{:S(2)}, u32[]{:S(2)}) async-start(bf16[32,8,1024]{2,1,0:T(8,128)(2,1)} %bitcast.3), calls=%async_computation | async-start | bytes 1048576 | tf_op jit(solution)/shard_map/all_to_all | solution.py:692
  34.1 6.8 %collective-permute-start = (s16[520,128]{1,0:T(8,128)(2,1)S(1)}, s16[520,128]{1,0:T(8,128)(2,1)S(1)}, u32[]{:S(2)}, u32[]{:S(2)}) collective-permute-start(s16[520,128]{1,0:T(8,128)(2,1)S(1)} %get-tuple-element.48), channel_id=1, source_target_pairs={{0,16},{4,20},{8,24},{12,28},{16,0},{20,4},{24,8},{28,12},{1,17},{... | collective-permute-start | bytes 399368 | tf_op jit(solution)/shard_map/ppermute | solution.py:695
  35.6 7.0 %collective-permute-start.1 = (s16[520,128]{1,0:T(8,128)(2,1)S(1)}, s16[520,128]{1,0:T(8,128)(2,1)S(1)}, u32[]{:S(2)}, u32[]{:S(2)}) collective-permute-start(s16[520,128]{1,0:T(8,128)(2,1)S(1)} %get-tuple-element.49), channel_id=1, source_target_pairs={{0,8},{4,12},{8,0},{12,4},{16,24},{20,28},{24,16},{28,20},{1,9},{5... | collective-permute-start | bytes 399368 | tf_op jit(solution)/shard_map/ppermute | solution.py:695
  36.8 12.1 %collective-permute-start.9 = (s16[520,128]{1,0:T(8,128)(2,1)}, s16[520,128]{1,0:T(8,128)(2,1)S(1)}, u32[]{:S(2)}, u32[]{:S(2)}) collective-permute-start(s16[520,128]{1,0:T(8,128)(2,1)} %get-tuple-element.63), channel_id=1, source_target_pairs={{0,20},{4,16},{8,28},{12,24},{16,4},{20,0},{24,12},{28,8},{1,21},{... | collective-permute-start | bytes 399368 | tf_op jit(solution)/shard_map/ppermute | solution.py:695
  37.9 12.3 %collective-permute-start.10 = (s16[520,128]{1,0:T(8,128)(2,1)}, s16[520,128]{1,0:T(8,128)(2,1)S(1)}, u32[]{:S(2)}, u32[]{:S(2)}) collective-permute-start(s16[520,128]{1,0:T(8,128)(2,1)} %get-tuple-element.64), channel_id=1, source_target_pairs={{0,12},{4,8},{8,4},{12,0},{16,28},{20,24},{24,20},{28,16},{1,13},{... | collective-permute-start | bytes 399368 | tf_op jit(solution)/shard_map/ppermute | solution.py:695
  37.9 12.5 %collective-permute-start.11 = (s16[520,128]{1,0:T(8,128)(2,1)S(1)}, s16[520,128]{1,0:T(8,128)(2,1)S(1)}, u32[]{:S(2)}, u32[]{:S(2)}) collective-permute-start(s16[520,128]{1,0:T(8,128)(2,1)S(1)} %get-tuple-element.65), channel_id=1, source_target_pairs={{0,4},{4,0},{8,12},{12,8},{16,20},{20,16},{24,28},{28,24},{1,5},{5... | collective-permute-start | bytes 399368 | tf_op jit(solution)/shard_map/ppermute | solution.py:695
  40.9 10.3 %collective-permute-start.12 = (s16[520,128]{1,0:T(8,128)(2,1)S(1)}, s16[520,128]{1,0:T(8,128)(2,1)S(1)}, u32[]{:S(2)}, u32[]{:S(2)}) collective-permute-start(s16[520,128]{1,0:T(8,128)(2,1)S(1)} %get-tuple-element.66), channel_id=1, source_target_pairs={{0,24},{4,28},{8,16},{12,20},{16,8},{20,12},{24,0},{28,4},{1,25},{... | collective-permute-start | bytes 399368 | tf_op jit(solution)/shard_map/ppermute | solution.py:695
  42.6 9.5 %collective-permute-start.13 = (s16[520,128]{1,0:T(8,128)(2,1)S(1)}, s16[520,128]{1,0:T(8,128)(2,1)S(1)}, u32[]{:S(2)}, u32[]{:S(2)}) collective-permute-start(s16[520,128]{1,0:T(8,128)(2,1)S(1)} %get-tuple-element.67), channel_id=1, source_target_pairs={{0,28},{4,24},{8,20},{12,16},{16,12},{20,8},{24,4},{28,0},{1,29},{... | collective-permute-start | bytes 399368 | tf_op jit(solution)/shard_map/ppermute | solution.py:695
  48.9 6.1 %collective-permute-start.4 = (s16[520,128]{1,0:T(8,128)(2,1)S(1)}, s16[520,128]{1,0:T(8,128)(2,1)S(1)}, u32[]{:S(2)}, u32[]{:S(2)}) collective-permute-start(s16[520,128]{1,0:T(8,128)(2,1)S(1)} %get-tuple-element.55), channel_id=1, source_target_pairs={{0,16},{4,20},{8,24},{12,28},{16,0},{20,4},{24,8},{28,12},{1,17},{... | collective-permute-start | bytes 399368 | tf_op jit(solution)/shard_map/ppermute | solution.py:695
  50.1 6.2 %collective-permute-start.5 = (s16[520,128]{1,0:T(8,128)(2,1)S(1)}, s16[520,128]{1,0:T(8,128)(2,1)S(1)}, u32[]{:S(2)}, u32[]{:S(2)}) collective-permute-start(s16[520,128]{1,0:T(8,128)(2,1)S(1)} %get-tuple-element.56), channel_id=1, source_target_pairs={{0,8},{4,12},{8,0},{12,4},{16,24},{20,28},{24,16},{28,20},{1,9},{5... | collective-permute-start | bytes 399368 | tf_op jit(solution)/shard_map/ppermute | solution.py:695
  50.4 9.2 %collective-permute-start.6 = (s16[520,128]{1,0:T(8,128)(2,1)S(1)}, s16[520,128]{1,0:T(8,128)(2,1)S(1)}, u32[]{:S(2)}, u32[]{:S(2)}) collective-permute-start(s16[520,128]{1,0:T(8,128)(2,1)S(1)} %get-tuple-element.57), channel_id=1, source_target_pairs={{0,20},{4,16},{8,28},{12,24},{16,4},{20,0},{24,12},{28,8},{1,21},{... | collective-permute-start | bytes 399368 | tf_op jit(solution)/shard_map/ppermute | solution.py:695
  51.3 8.4 %collective-permute-start.7 = (s16[520,128]{1,0:T(8,128)(2,1)S(1)}, s16[520,128]{1,0:T(8,128)(2,1)S(1)}, u32[]{:S(2)}, u32[]{:S(2)}) collective-permute-start(s16[520,128]{1,0:T(8,128)(2,1)S(1)} %get-tuple-element.58), channel_id=1, source_target_pairs={{0,12},{4,8},{8,4},{12,0},{16,28},{20,24},{24,20},{28,16},{1,13},{... | collective-permute-start | bytes 399368 | tf_op jit(solution)/shard_map/ppermute | solution.py:695
  52.1 7.5 %collective-permute-start.8 = (s16[520,128]{1,0:T(8,128)(2,1)S(1)}, s16[520,128]{1,0:T(8,128)(2,1)S(1)}, u32[]{:S(2)}, u32[]{:S(2)}) collective-permute-start(s16[520,128]{1,0:T(8,128)(2,1)S(1)} %get-tuple-element.59), channel_id=1, source_target_pairs={{0,4},{4,0},{8,12},{12,8},{16,20},{20,16},{24,28},{28,24},{1,5},{5... | collective-permute-start | bytes 399368 | tf_op jit(solution)/shard_map/ppermute | solution.py:695
  54.9 6.5 %collective-permute-start.2 = (s16[520,128]{1,0:T(8,128)(2,1)S(1)}, s16[520,128]{1,0:T(8,128)(2,1)S(1)}, u32[]{:S(2)}, u32[]{:S(2)}) collective-permute-start(s16[520,128]{1,0:T(8,128)(2,1)S(1)} %get-tuple-element.52), channel_id=1, source_target_pairs={{0,24},{4,28},{8,16},{12,20},{16,8},{20,12},{24,0},{28,4},{1,25},{... | collective-permute-start | bytes 399368 | tf_op jit(solution)/shard_map/ppermute | solution.py:695
  56.4 7.6 %collective-permute-start.3 = (s16[520,128]{1,0:T(8,128)(2,1)S(1)}, s16[520,128]{1,0:T(8,128)(2,1)S(1)}, u32[]{:S(2)}, u32[]{:S(2)}) collective-permute-start(s16[520,128]{1,0:T(8,128)(2,1)S(1)} %get-tuple-element.53), channel_id=1, source_target_pairs={{0,28},{4,24},{8,20},{12,16},{16,12},{20,8},{24,4},{28,0},{1,29},{... | collective-permute-start | bytes 399368 | tf_op jit(solution)/shard_map/ppermute | solution.py:695
  66.1 6.9 %collective-permute-start.16 = (s16[136,128]{1,0:T(8,128)(2,1)S(1)}, s16[136,128]{1,0:T(8,128)(2,1)S(1)}, u32[]{:S(2)}, u32[]{:S(2)}) collective-permute-start(s16[136,128]{1,0:T(8,128)(2,1)S(1)} %get-tuple-element.73.refs_0_), channel_id=1, source_target_pairs={{0,3},{1,0},{2,1},{3,2},{4,7},{5,4},{6,5},{7,6},{8,11},{9,8},{10,9... | collective-permute-start | bytes 104456 | tf_op jit(solution)/shard_map/ppermute | solution.py:698
  77.9 6.5 %collective-permute-start.19 = (s16[1032,128]{1,0:T(8,128)(2,1)S(1)}, s16[1032,128]{1,0:T(8,128)(2,1)S(1)}, u32[]{:S(2)}, u32[]{:S(2)}) collective-permute-start(s16[1032,128]{1,0:T(8,128)(2,1)S(1)} %get-tuple-element.77), channel_id=1, source_target_pairs={{0,16},{4,20},{8,24},{12,28},{16,0},{20,4},{24,8},{28,12},{1,17},{... | collective-permute-start | bytes 792584 | tf_op jit(solution)/shard_map/ppermute | solution.py:695
  78.8 6.9 %collective-permute-start.20 = (s16[1032,128]{1,0:T(8,128)(2,1)S(1)}, s16[1032,128]{1,0:T(8,128)(2,1)S(1)}, u32[]{:S(2)}, u32[]{:S(2)}) collective-permute-start(s16[1032,128]{1,0:T(8,128)(2,1)S(1)} %get-tuple-element.78), channel_id=1, source_target_pairs={{0,8},{4,12},{8,0},{12,4},{16,24},{20,28},{24,16},{28,20},{1,9},{5... | collective-permute-start | bytes 792584 | tf_op jit(solution)/shard_map/ppermute | solution.py:695
  79.6 13.1 %collective-permute-start.21 = (s16[1032,128]{1,0:T(8,128)(2,1)S(1)}, s16[1032,128]{1,0:T(8,128)(2,1)S(1)}, u32[]{:S(2)}, u32[]{:S(2)}) collective-permute-start(s16[1032,128]{1,0:T(8,128)(2,1)S(1)} %get-tuple-element.79), channel_id=1, source_target_pairs={{0,20},{4,16},{8,28},{12,24},{16,4},{20,0},{24,12},{28,8},{1,21},{... | collective-permute-start | bytes 792584 | tf_op jit(solution)/shard_map/ppermute | solution.py:695
  82.3 12.7 %collective-permute-start.22 = (s16[1032,128]{1,0:T(8,128)(2,1)S(1)}, s16[1032,128]{1,0:T(8,128)(2,1)S(1)}, u32[]{:S(2)}, u32[]{:S(2)}) collective-permute-start(s16[1032,128]{1,0:T(8,128)(2,1)S(1)} %get-tuple-element.80), channel_id=1, source_target_pairs={{0,12},{4,8},{8,4},{12,0},{16,28},{20,24},{24,20},{28,16},{1,13},{... | collective-permute-start | bytes 792584 | tf_op jit(solution)/shard_map/ppermute | solution.py:695
  82.4 12.6 %collective-permute-start.23 = (s16[1032,128]{1,0:T(8,128)(2,1)S(1)}, s16[1032,128]{1,0:T(8,128)(2,1)S(1)}, u32[]{:S(2)}, u32[]{:S(2)}) collective-permute-start(s16[1032,128]{1,0:T(8,128)(2,1)S(1)} %get-tuple-element.81), channel_id=1, source_target_pairs={{0,4},{4,0},{8,12},{12,8},{16,20},{20,16},{24,28},{28,24},{1,5},{5... | collective-permute-start | bytes 792584 | tf_op jit(solution)/shard_map/ppermute | solution.py:695
  84.5 14.9 %collective-permute-start.17 = (s16[1032,128]{1,0:T(8,128)(2,1)S(1)}, s16[1032,128]{1,0:T(8,128)(2,1)S(1)}, u32[]{:S(2)}, u32[]{:S(2)}) collective-permute-start(s16[1032,128]{1,0:T(8,128)(2,1)S(1)} %get-tuple-element.74), channel_id=1, source_target_pairs={{0,24},{4,28},{8,16},{12,20},{16,8},{20,12},{24,0},{28,4},{1,25},{... | collective-permute-start | bytes 792584 | tf_op jit(solution)/shard_map/ppermute | solution.py:695
  85.7 18.5 %collective-permute-start.18 = (s16[1032,128]{1,0:T(8,128)(2,1)S(1)}, s16[1032,128]{1,0:T(8,128)(2,1)S(1)}, u32[]{:S(2)}, u32[]{:S(2)}) collective-permute-start(s16[1032,128]{1,0:T(8,128)(2,1)S(1)} %get-tuple-element.75), channel_id=1, source_target_pairs={{0,28},{4,24},{8,20},{12,16},{16,12},{20,8},{24,4},{28,0},{1,29},{... | collective-permute-start | bytes 792584 | tf_op jit(solution)/shard_map/ppermute | solution.py:695
  (12 other events, 294.7 us)
where the time goes:
time: 138 us
  starting transfers between devices  39.9 us (29%)
  waiting for transfers between devices  33.2 us (24%)
  Pallas kernels  31.9 us (23%)
  blocking collectives  29.7 us (22%)
  local copies, waits for them, and re-layouts  1.91 us (1%)
    pallas_call x12, Pallas kernels, call(): pl.pallas_call(kernel, out_shape=outs, in_specs=[pl.BlockSpec(memory_spac...  31.9 us
    all_to_all x1, blocking collectives, all_ways(): lax.all_to_all(values, ('gz', 'ma'), split_axis=0, concat_axis=0, tiled=T...  29.7 us
    ppermute x21, starting transfers between devices, over_slabs(): lax.ppermute(values, 'gz', [(g, g ^ offset) for g in range(SLABS)])  25.8 us
    ppermute x21, waiting for transfers between devices, over_slabs(): lax.ppermute(values, 'gz', [(g, g ^ offset) for g in range(SLABS)])  18 us
    all_to_all x2, waiting for transfers between devices, all_ways(): lax.all_to_all(values, ('gz', 'ma'), split_axis=0, concat_axis=0, tiled=T...  14.8 us
    all_to_all x2, starting transfers between devices, all_ways(): lax.all_to_all(values, ('gz', 'ma'), split_axis=0, concat_axis=0, tiled=T...  10.3 us
    ppermute x3, starting transfers between devices, round_groups(): lax.ppermute(values, 'ma', [(m, (m + step) % GROUPS) for m in range(GROUP...  3.89 us
  transfers between devices with their start and end apart: 26, of which 10 were waited for; matrix products, arithmetic and copies ran while one was open for 0% of the time, Pallas kernels for 14%

commit v1 on v0

--- a/solution.py
+++ b/solution.py
@@ -224,7 +224,8 @@
     for own in range(SLABS):
         slabs = np.array([own ^ offset for offset in offsets])
         plane, tz = np.array(planes)[:, None, None], np.arange(BZ)[None, :, None]
-        part = table[:, (slabs * CZ + tz * BZ + plane).reshape(-1)]
+        place = slabs * CZ + tz * BZ + plane
+        part = table[:, (place.transpose(0, 2, 1) if turned else place).reshape(-1)]
         high, low = split_table(part.T if turned else part)
         if turned or 3 * high.shape[1] <= 2 * LANES:
             each.append(np.concatenate([high, high, low], axis=1))
@@ -557,7 +558,7 @@
     end_refs, plane_ref = refs[:GROUPS], refs[GROUPS].at[own_ref[0]]
     count = GROUPS + 1 + len(SEND)
     sent_refs = refs[GROUPS + 1 : count]
-    rise_ref, fall_ref, grid_ref, level_ref = refs[count:]
+    rise_ref, fall_ref, lines_ref = refs[count:]
     low = low_half((PLANES, LANES))
     root = root_ref[...]
     square = root * root
@@ -576,25 +577,35 @@
     rise_ref[...] = jnp.where(low, turned, straight)
     fall_ref[...] = jnp.where(low, straight, turned)
     slabs = len(sent_refs)
+    upper = lax.broadcasted_iota(jnp.int32, (8, LANES), 0) < 4
 
     def solved(step):
         reach = rise_ref[...] * power_ref[step] + fall_ref[...] * power_ref[STEPS - 1 - step]
         return local_ref[step] + reach
 
-    def sines(tx, most):
-        lines = plane_product(plane_ref, jnp.concatenate([solved(tx * 4 + xq) for xq in range(4)], axis=1))
+    def lines_of(tx):
+        return plane_product(plane_ref, jnp.concatenate([solved(tx * 4 + xq) for xq in range(4)], axis=1))
+
+    def sines(step, most):
+        most = list(most)
+        both = lines_of(2 * step), lines_of(2 * step + 1)
         for xq in range(4):
-            part = lines[:, xq * LANES : (xq + 1) * LANES]
-            most = jnp.maximum(most, jnp.max(jnp.abs(part).reshape(4 * BZ, slabs, LANES), axis=0))
+            there = slice(xq * LANES, (xq + 1) * LANES)
             for plane in range(BZ):
-                grid_ref[grid_rows(slabs, plane, xq, tx), :] = part[plane * 4 * slabs : (plane + 1) * 4 * slabs]
-        return most
-
-    most = lax.fori_loop(0, 16, sines, jnp.zeros((slabs, LANES), jnp.float32), unroll=8)
-    level_ref[...] = level_of(most)
+                row = pl.multiple_of((plane * 4 + xq) * SPOTS + step * 8, 8)
+                for slab in range(0, slabs, 2):
+                    start = plane * 4 * slabs + slab * 4
+                    first, second = (each[start : start + 8, there] for each in both)
+                    crossed = pltpu.roll(jnp.where(upper, second, first), 4, 0)
+                    for one, values in enumerate((jnp.where(upper, first, crossed), jnp.where(upper, crossed, second))):
+                        lines_ref[slab + one, pl.ds(row, 8), :] = values
+                        most[slab + one] = jnp.maximum(most[slab + one], jnp.abs(values))
+        return tuple(most)
+
+    most = lax.fori_loop(0, 8, sines, (jnp.zeros((8, LANES), jnp.float32),) * slabs, unroll=4)
     for at, sent_ref in enumerate(sent_refs):
-        level = level_ref[at : at + 1, :]
-        sent_ref[:ROWS, :] = fixed_of(grid_ref[pl.ds(at, ROWS, stride=slabs), :] * inverse_of(level))
+        level = level_of(jnp.max(most[at], axis=0, keepdims=True))
+        sent_ref[:ROWS, :] = fixed_of(lines_ref[at] * inverse_of(level))
         sent_ref[ROWS:, :] = head_of(level)
 
 
@@ -802,8 +813,7 @@
         [
             V(flat, f32),
             V(flat, f32),
-            V((len(SEND) * ROWS, LANES), f32),
-            V((len(SEND), LANES), f32),
+            V((len(SEND), ROWS, LANES), f32),
         ],
     )
     got = exchanged(sent)

time: 138 us -> 137 us (level)
  no operation moved by 1% of the time
where the time goes in v1:
time: 137 us
  starting transfers between devices  39.9 us (29%)
  waiting for transfers between devices  33.2 us (24%)
  Pallas kernels  31 us (23%)
  blocking collectives  29.7 us (22%)
  local copies, waits for them, and re-layouts  1.91 us (1%)
    pallas_call x12, Pallas kernels, call(): pl.pallas_call(kernel, out_shape=outs, in_specs=[pl.BlockSpec(memory_spac...  31 us
    all_to_all x1, blocking collectives, all_ways(): lax.all_to_all(values, ('gz', 'ma'), split_axis=0, concat_axis=0, tiled=T...  29.7 us
    ppermute x21, starting transfers between devices, over_slabs(): lax.ppermute(values, 'gz', [(g, g ^ offset) for g in range(SLABS)])  25.8 us
    ppermute x21, waiting for transfers between devices, over_slabs(): lax.ppermute(values, 'gz', [(g, g ^ offset) for g in range(SLABS)])  18 us
    all_to_all x2, waiting for transfers between devices, all_ways(): lax.all_to_all(values, ('gz', 'ma'), split_axis=0, concat_axis=0, tiled=T...  14.8 us
    all_to_all x2, starting transfers between devices, all_ways(): lax.all_to_all(values, ('gz', 'ma'), split_axis=0, concat_axis=0, tiled=T...  10.3 us
    ppermute x3, starting transfers between devices, round_groups(): lax.ppermute(values, 'ma', [(m, (m + step) % GROUPS) for m in range(GROUP...  3.89 us
  transfers between devices with their start and end apart: 26, of which 10 were waited for; matrix products, arithmetic and copies ran while one was open for 0% of the time, Pallas kernels for 14%

profile of v1, /device:TPU:1, one launch (start us, length us, event | category | flops | bytes accessed | tf_op | source)
XLA Modules:
  0.0 136.8 jit_solution(1663499598542789492)
XLA Ops:
  0.8 2.7 %pack.1 = (bf16[256,1152]{1,0:T(8,128)(2,1)}, bf16[256,128]{1,0:T(8,128)(2,1)}) custom-call(s32[1,128]{1,0:T(1,128)} %bitcast.14, s32[1,128]{1,0:T(1,128)} %bitcast.15, s32[1]{0:T(128)S(6)} %copy.14.count_in, bf16[128,2048]{1,0:T(8,128)(2,1)} %brick_in.3), custom_call_target="tpu_custom_call" | custom-call | tf_op jit(solution)/shard_map/pack/pallas_call | solution.py:670
  3.5 7.1 %all-to-all-start.1 = ((bf16[32,8,1152]{2,1,0:T(8,128)(2,1)}), bf16[32,8,1152]{2,1,0:T(8,128)(2,1)S(1)}, u32[]{:S(2)}, u32[]{:S(2)}) async-start(bf16[32,8,1152]{2,1,0:T(8,128)(2,1)} %bitcast.13), calls=%async_computation.1 | async-start | bytes 1179648 | tf_op jit(solution)/shard_map/all_to_all | solution.py:703
  13.7 13.6 %all-to-all-done.1 = bf16[32,8,1152]{2,1,0:T(8,128)(2,1)S(1)} async-done(((bf16[32,8,1152]{2,1,0:T(8,128)(2,1)}), bf16[32,8,1152]{2,1,0:T(8,128)(2,1)S(1)}, u32[]{:S(2)}, u32[]{:S(2)}) %all-to-all-start.1) | async-done | bytes 589856 | tf_op jit(solution)/shard_map/all_to_all | solution.py:703
  27.3 3.2 %all-to-all-start = ((bf16[32,8,1024]{2,1,0:T(8,128)(2,1)}), bf16[32,8,1024]{2,1,0:T(8,128)(2,1)S(1)}, u32[]{:S(2)}, u32[]{:S(2)}) async-start(bf16[32,8,1024]{2,1,0:T(8,128)(2,1)} %bitcast.3), calls=%async_computation | async-start | bytes 1048576 | tf_op jit(solution)/shard_map/all_to_all | solution.py:703
  30.4 3.7 %forward_first.1 = (s16[520,128]{1,0:T(8,128)(2,1)S(1)}, s16[520,128]{1,0:T(8,128)(2,1)S(1)}, s16[520,128]{1,0:T(8,128)(2,1)}, s16[520,128]{1,0:T(8,128)(2,1)}, ...) custom-call(s32[1]{0:T(128)} %bitcast.2.own_ref, ...), custom_call_target="tpu_custom_call" | custom-call | tf_op jit(solution)/shard_map/forward_first/pallas_call | solution.py:670
  38.2 2.7 %collective-permute-done.refs_1_ = s16[520,128]{1,0:T(8,128)(2,1)S(1)} collective-permute-done((s16[520,128]{1,0:T(8,128)(2,1)S(1)}, s16[520,128]{1,0:T(8,128)(2,1)S(1)}, u32[]{:S(2)}, u32[]{:S(2)}) %collective-permute-start) | collective-permute-done | bytes 133152 | tf_op jit(solution)/shard_map/ppermute | solution.py:706
  40.9 1.7 %collective-permute-start.12 = (s16[520,128]{1,0:T(8,128)(2,1)S(1)}, s16[520,128]{1,0:T(8,128)(2,1)S(1)}, u32[]{:S(2)}, u32[]{:S(2)}) collective-permute-start(s16[520,128]{1,0:T(8,128)(2,1)S(1)} %get-tuple-element.66), channel_id=1, source_target_pairs={{0,24},{4,28},{8,16},{12,20},{16,8},{20,12},{24,0},{28,4},{1,25},{... | collective-permute-start | bytes 399368 | tf_op jit(solution)/shard_map/ppermute | solution.py:706
  42.6 2.0 %collective-permute-start.13 = (s16[520,128]{1,0:T(8,128)(2,1)S(1)}, s16[520,128]{1,0:T(8,128)(2,1)S(1)}, u32[]{:S(2)}, u32[]{:S(2)}) collective-permute-start(s16[520,128]{1,0:T(8,128)(2,1)S(1)} %get-tuple-element.67), channel_id=1, source_target_pairs={{0,28},{4,24},{8,20},{12,16},{16,12},{20,8},{24,4},{28,0},{1,29},{... | collective-permute-start | bytes 399368 | tf_op jit(solution)/shard_map/ppermute | solution.py:706
  45.8 3.0 %forward_later.1 = (s16[520,128]{1,0:T(8,128)(2,1)S(1)}, s16[520,128]{1,0:T(8,128)(2,1)S(1)}, s16[520,128]{1,0:T(8,128)(2,1)S(1)}, s16[520,128]{1,0:T(8,128)(2,1...) custom-call(s32[1]{0:T(128)} %bitcast.2.own_ref, ...), custom_call_target="tpu_custom_call" | custom-call | tf_op jit(solution)/shard_map/forward_later/pallas_call | solution.py:670
  52.2 2.8 %collective-permute-done.4.refs_1_ = s16[520,128]{1,0:T(8,128)(2,1)S(1)} collective-permute-done((s16[520,128]{1,0:T(8,128)(2,1)S(1)}, s16[520,128]{1,0:T(8,128)(2,1)S(1)}, u32[]{:S(2)}, u32[]{:S(2)}) %collective-permute-start.4) | collective-permute-done | bytes 133152 | tf_op jit(solution)/shard_map/ppermute | solution.py:706
  57.8 1.8 %down_first.1 = (f32[64,128,128]{2,1,0:T(8,128)S(1)}, f32[128,128]{1,0:T(8,128)S(1)}, f32[128,128]{1,0:T(8,128)S(1)}, f32[64,128,128]{2,1,0:T(8,128)S(1)}) custom-call(s32[1]{0:T(128)} %bitcast.2.own_ref, s16[520,128]{1,0:T(8,128)(2,1)S(1)} %get-tuple-element.60.refs_0_, s16[520,128]{1,0:T(8,128)(2,1)S(1)} %collective-permute-done.refs_1_, ...), custom_call_target="tpu_custom_call" | custom-call | tf_op jit(solution)/shard_map/down_first/pallas_call | solution.py:670
  59.7 1.7 %down_middle.1.refs_2_ = f32[64,128,128]{2,1,0:T(8,128)S(1)} custom-call(s32[1]{0:T(128)} %bitcast.2.own_ref, s16[520,128]{1,0:T(8,128)(2,1)S(1)} %get-tuple-element.54.refs_0_, s16[520,128]{1,0:T(8,128)(2,1)S(1)} %collective-permute-done.4.refs_1_, s16[520,128]{1,0:T(8,128)(2,1)S(1)} %collective-permute-done.5.refs_2_, ...), custom_call_target="tpu_custom_call" | custom-call | tf_op jit(solution)/shard_map/down_middle/pallas_call | solution.py:670
  61.5 2.5 %collective-permute-done.3.refs_1_ = s16[520,128]{1,0:T(8,128)(2,1)S(1)} collective-permute-done((s16[520,128]{1,0:T(8,128)(2,1)S(1)}, s16[520,128]{1,0:T(8,128)(2,1)S(1)}, u32[]{:S(2)}, u32[]{:S(2)}) %collective-permute-start.3) | collective-permute-done | bytes 133152 | tf_op jit(solution)/shard_map/ppermute | solution.py:706
  63.9 2.1 %down_later.1 = (f32[64,128,128]{2,1,0:T(8,128)S(1)}, s16[136,128]{1,0:T(8,128)(2,1)S(1)}) custom-call(s32[1]{0:T(128)} %bitcast.2.own_ref, s16[520,128]{1,0:T(8,128)(2,1)S(1)} %collective-permute-done.2.refs_0_, s16[520,128]{1,0:T(8,128)(2,1)S(1)} %collective-permute-done.3.refs_1_, f32[64,128,128]{2,1,0:T(8,128)S(1)} %down_middle.1.refs_2_, ...), custom_call_target="tpu_custom_call" | custom-call | tf_op jit(solution)/shard_map/down_later/pallas_call | solution.py:670
  66.1 2.6 %collective-permute-start.16 = (s16[136,128]{1,0:T(8,128)(2,1)S(1)}, s16[136,128]{1,0:T(8,128)(2,1)S(1)}, u32[]{:S(2)}, u32[]{:S(2)}) collective-permute-start(s16[136,128]{1,0:T(8,128)(2,1)S(1)} %get-tuple-element.73.refs_0_), channel_id=1, source_target_pairs={{0,3},{1,0},{2,1},{3,2},{4,7},{5,4},{6,5},{7,6},{8,11},{9,8},{10,9... | collective-permute-start | bytes 104456 | tf_op jit(solution)/shard_map/ppermute | solution.py:709
  69.9 3.0 %local.1.local_ref = f32[64,128,128]{2,1,0:T(8,128)S(1)} custom-call(f32[64,128,128]{2,1,0:T(8,128)S(1)} %get-tuple-element.70.walk_ref, f32[128,128]{1,0:T(8,128)S(1)} %get-tuple-element.69.refs_7_.refs_3_.root_ref, f32[128,128]{1,0:T(8,128)S(1)} %get-tuple-element.71.gain_ref), custom_call_target="tpu_custom_call" | custom-call | tf_op jit(solution)/shard_map/local/pallas_call | solution.py:670
  73.4 3.6 %up.1 = (s16[1032,128]{1,0:T(8,128)(2,1)S(1)}, s16[1032,128]{1,0:T(8,128)(2,1)S(1)}, s16[1032,128]{1,0:T(8,128)(2,1)S(1)}, s16[1032,128]{1,0:T(8,128)(2,1)S(1)},...) custom-call(s32[1]{0:T(128)} %bitcast.2.own_ref, ...), custom_call_target="tpu_custom_call" | custom-call | tf_op jit(solution)/shard_map/up/pallas_call | solution.py:670
  78.8 2.7 %collective-permute-start.21 = (s16[1032,128]{1,0:T(8,128)(2,1)S(1)}, s16[1032,128]{1,0:T(8,128)(2,1)S(1)}, u32[]{:S(2)}, u32[]{:S(2)}) collective-permute-start(s16[1032,128]{1,0:T(8,128)(2,1)S(1)} %get-tuple-element.79), channel_id=1, source_target_pairs={{0,20},{4,16},{8,28},{12,24},{16,4},{20,0},{24,12},{28,8},{1,21},{... | collective-permute-start | bytes 792584 | tf_op jit(solution)/shard_map/ppermute | solution.py:706
  84.8 5.5 %collective-permute-start.18 = (s16[1032,128]{1,0:T(8,128)(2,1)S(1)}, s16[1032,128]{1,0:T(8,128)(2,1)S(1)}, u32[]{:S(2)}, u32[]{:S(2)}) collective-permute-start(s16[1032,128]{1,0:T(8,128)(2,1)S(1)} %get-tuple-element.75), channel_id=1, source_target_pairs={{0,28},{4,24},{8,20},{12,16},{16,12},{20,8},{24,4},{28,0},{1,29},{... | collective-permute-start | bytes 792584 | tf_op jit(solution)/shard_map/ppermute | solution.py:706
  91.9 2.3 %collective-permute-done.22.refs_4_ = s16[1032,128]{1,0:T(8,128)(2,1)S(1)} collective-permute-done((s16[1032,128]{1,0:T(8,128)(2,1)S(1)}, s16[1032,128]{1,0:T(8,128)(2,1)S(1)}, u32[]{:S(2)}, u32[]{:S(2)}) %collective-permute-start.22) | collective-permute-done | bytes 264224 | tf_op jit(solution)/shard_map/ppermute | solution.py:706
  94.1 4.4 %reply_first.1.refs_2_ = f32[8,1024,128]{2,1,0:T(8,128)S(1)} custom-call(s32[1]{0:T(128)} %bitcast.2.own_ref, f32[4,12]{1,0:T(4,128)S(1)} %copy-done.8, s16[1032,128]{1,0:T(8,128)(2,1)S(1)} %get-tuple-element.76.refs_0_, s16[1032,128]{1,0:T(8,128)(2,1)S(1)} %collective-permute-done.19.refs_1_, s16[1032,128]{1,0:T(8,128)(2,1)S(1)} %collective-permute-done.20.refs_2_, ...), custom_call_target="tpu_custom_call" | custom-call | tf_op jit(solution)/shard_map/reply_first/pallas_call | solution.py:670
  98.5 4.8 %collective-permute-done.18.refs_1_ = s16[1032,128]{1,0:T(8,128)(2,1)S(1)} collective-permute-done((s16[1032,128]{1,0:T(8,128)(2,1)S(1)}, s16[1032,128]{1,0:T(8,128)(2,1)S(1)}, u32[]{:S(2)}, u32[]{:S(2)}) %collective-permute-start.18) | collective-permute-done | bytes 264224 | tf_op jit(solution)/shard_map/ppermute | solution.py:706
  103.4 2.6 %reply_later.1 = bf16[256,2048]{1,0:T(8,128)(2,1)S(1)} custom-call(s32[1]{0:T(128)} %bitcast.2.own_ref, f32[4,12]{1,0:T(4,128)S(1)} %copy-done.8, s16[1032,128]{1,0:T(8,128)(2,1)S(1)} %collective-permute-done.17.refs_0_, s16[1032,128]{1,0:T(8,128)(2,1)S(1)} %collective-permute-done.18.refs_1_, f32[8,1024,128]{2,1,0:T(8,128)S(1)} %reply_first.1.refs_2_, ...), custom_call_target="tpu_custom_call" | custom-call | tf_op jit(solution)/shard_map/reply_later/pallas_call | solution.py:670
  106.0 29.7 %all_to_all.34 = bf16[32,8,2048]{2,1,0:T(8,128)(2,1)S(1)} all-to-all(bf16[32,8,2048]{2,1,0:T(8,128)(2,1)S(1)} %bitcast.10), channel_id=1, replica_groups=mesh['gz'=8,'ma'=4] {'gz','ma'}, dimensions={0} | all-to-all | bytes 2097152 | tf_op jit(solution)/shard_map/all_to_all | solution.py:703
  (61 shorter events, 24.2 us)
Async XLA Ops:
  3.5 23.8 %all-to-all-start.1 = ((bf16[32,8,1152]{2,1,0:T(8,128)(2,1)}), bf16[32,8,1152]{2,1,0:T(8,128)(2,1)S(1)}, u32[]{:S(2)}, u32[]{:S(2)}) async-start(bf16[32,8,1152]{2,1,0:T(8,128)(2,1)} %bitcast.13), calls=%async_computation.1 | async-start | bytes 1179648 | tf_op jit(solution)/shard_map/all_to_all | solution.py:703
  27.3 18.6 %all-to-all-start = ((bf16[32,8,1024]{2,1,0:T(8,128)(2,1)}), bf16[32,8,1024]{2,1,0:T(8,128)(2,1)S(1)}, u32[]{:S(2)}, u32[]{:S(2)}) async-start(bf16[32,8,1024]{2,1,0:T(8,128)(2,1)} %bitcast.3), calls=%async_computation | async-start | bytes 1048576 | tf_op jit(solution)/shard_map/all_to_all | solution.py:703
  34.1 6.8 %collective-permute-start = (s16[520,128]{1,0:T(8,128)(2,1)S(1)}, s16[520,128]{1,0:T(8,128)(2,1)S(1)}, u32[]{:S(2)}, u32[]{:S(2)}) collective-permute-start(s16[520,128]{1,0:T(8,128)(2,1)S(1)} %get-tuple-element.48), channel_id=1, source_target_pairs={{0,16},{4,20},{8,24},{12,28},{16,0},{20,4},{24,8},{28,12},{1,17},{... | collective-permute-start | bytes 399368 | tf_op jit(solution)/shard_map/ppermute | solution.py:706
  35.6 7.0 %collective-permute-start.1 = (s16[520,128]{1,0:T(8,128)(2,1)S(1)}, s16[520,128]{1,0:T(8,128)(2,1)S(1)}, u32[]{:S(2)}, u32[]{:S(2)}) collective-permute-start(s16[520,128]{1,0:T(8,128)(2,1)S(1)} %get-tuple-element.49), channel_id=1, source_target_pairs={{0,8},{4,12},{8,0},{12,4},{16,24},{20,28},{24,16},{28,20},{1,9},{5... | collective-permute-start | bytes 399368 | tf_op jit(solution)/shard_map/ppermute | solution.py:706
  36.8 12.1 %collective-permute-start.9 = (s16[520,128]{1,0:T(8,128)(2,1)}, s16[520,128]{1,0:T(8,128)(2,1)S(1)}, u32[]{:S(2)}, u32[]{:S(2)}) collective-permute-start(s16[520,128]{1,0:T(8,128)(2,1)} %get-tuple-element.63), channel_id=1, source_target_pairs={{0,20},{4,16},{8,28},{12,24},{16,4},{20,0},{24,12},{28,8},{1,21},{... | collective-permute-start | bytes 399368 | tf_op jit(solution)/shard_map/ppermute | solution.py:706
  37.9 12.3 %collective-permute-start.10 = (s16[520,128]{1,0:T(8,128)(2,1)}, s16[520,128]{1,0:T(8,128)(2,1)S(1)}, u32[]{:S(2)}, u32[]{:S(2)}) collective-permute-start(s16[520,128]{1,0:T(8,128)(2,1)} %get-tuple-element.64), channel_id=1, source_target_pairs={{0,12},{4,8},{8,4},{12,0},{16,28},{20,24},{24,20},{28,16},{1,13},{... | collective-permute-start | bytes 399368 | tf_op jit(solution)/shard_map/ppermute | solution.py:706
  37.9 12.5 %collective-permute-start.11 = (s16[520,128]{1,0:T(8,128)(2,1)S(1)}, s16[520,128]{1,0:T(8,128)(2,1)S(1)}, u32[]{:S(2)}, u32[]{:S(2)}) collective-permute-start(s16[520,128]{1,0:T(8,128)(2,1)S(1)} %get-tuple-element.65), channel_id=1, source_target_pairs={{0,4},{4,0},{8,12},{12,8},{16,20},{20,16},{24,28},{28,24},{1,5},{5... | collective-permute-start | bytes 399368 | tf_op jit(solution)/shard_map/ppermute | solution.py:706
  40.9 10.3 %collective-permute-start.12 = (s16[520,128]{1,0:T(8,128)(2,1)S(1)}, s16[520,128]{1,0:T(8,128)(2,1)S(1)}, u32[]{:S(2)}, u32[]{:S(2)}) collective-permute-start(s16[520,128]{1,0:T(8,128)(2,1)S(1)} %get-tuple-element.66), channel_id=1, source_target_pairs={{0,24},{4,28},{8,16},{12,20},{16,8},{20,12},{24,0},{28,4},{1,25},{... | collective-permute-start | bytes 399368 | tf_op jit(solution)/shard_map/ppermute | solution.py:706
  42.6 9.5 %collective-permute-start.13 = (s16[520,128]{1,0:T(8,128)(2,1)S(1)}, s16[520,128]{1,0:T(8,128)(2,1)S(1)}, u32[]{:S(2)}, u32[]{:S(2)}) collective-permute-start(s16[520,128]{1,0:T(8,128)(2,1)S(1)} %get-tuple-element.67), channel_id=1, source_target_pairs={{0,28},{4,24},{8,20},{12,16},{16,12},{20,8},{24,4},{28,0},{1,29},{... | collective-permute-start | bytes 399368 | tf_op jit(solution)/shard_map/ppermute | solution.py:706
  48.9 6.1 %collective-permute-start.4 = (s16[520,128]{1,0:T(8,128)(2,1)S(1)}, s16[520,128]{1,0:T(8,128)(2,1)S(1)}, u32[]{:S(2)}, u32[]{:S(2)}) collective-permute-start(s16[520,128]{1,0:T(8,128)(2,1)S(1)} %get-tuple-element.55), channel_id=1, source_target_pairs={{0,16},{4,20},{8,24},{12,28},{16,0},{20,4},{24,8},{28,12},{1,17},{... | collective-permute-start | bytes 399368 | tf_op jit(solution)/shard_map/ppermute | solution.py:706
  50.1 6.2 %collective-permute-start.5 = (s16[520,128]{1,0:T(8,128)(2,1)S(1)}, s16[520,128]{1,0:T(8,128)(2,1)S(1)}, u32[]{:S(2)}, u32[]{:S(2)}) collective-permute-start(s16[520,128]{1,0:T(8,128)(2,1)S(1)} %get-tuple-element.56), channel_id=1, source_target_pairs={{0,8},{4,12},{8,0},{12,4},{16,24},{20,28},{24,16},{28,20},{1,9},{5... | collective-permute-start | bytes 399368 | tf_op jit(solution)/shard_map/ppermute | solution.py:706
  50.4 9.2 %collective-permute-start.6 = (s16[520,128]{1,0:T(8,128)(2,1)S(1)}, s16[520,128]{1,0:T(8,128)(2,1)S(1)}, u32[]{:S(2)}, u32[]{:S(2)}) collective-permute-start(s16[520,128]{1,0:T(8,128)(2,1)S(1)} %get-tuple-element.57), channel_id=1, source_target_pairs={{0,20},{4,16},{8,28},{12,24},{16,4},{20,0},{24,12},{28,8},{1,21},{... | collective-permute-start | bytes 399368 | tf_op jit(solution)/shard_map/ppermute | solution.py:706
  51.3 8.4 %collective-permute-start.7 = (s16[520,128]{1,0:T(8,128)(2,1)S(1)}, s16[520,128]{1,0:T(8,128)(2,1)S(1)}, u32[]{:S(2)}, u32[]{:S(2)}) collective-permute-start(s16[520,128]{1,0:T(8,128)(2,1)S(1)} %get-tuple-element.58), channel_id=1, source_target_pairs={{0,12},{4,8},{8,4},{12,0},{16,28},{20,24},{24,20},{28,16},{1,13},{... | collective-permute-start | bytes 399368 | tf_op jit(solution)/shard_map/ppermute | solution.py:706
  52.1 7.5 %collective-permute-start.8 = (s16[520,128]{1,0:T(8,128)(2,1)S(1)}, s16[520,128]{1,0:T(8,128)(2,1)S(1)}, u32[]{:S(2)}, u32[]{:S(2)}) collective-permute-start(s16[520,128]{1,0:T(8,128)(2,1)S(1)} %get-tuple-element.59), channel_id=1, source_target_pairs={{0,4},{4,0},{8,12},{12,8},{16,20},{20,16},{24,28},{28,24},{1,5},{5... | collective-permute-start | bytes 399368 | tf_op jit(solution)/shard_map/ppermute | solution.py:706
  54.9 6.5 %collective-permute-start.2 = (s16[520,128]{1,0:T(8,128)(2,1)S(1)}, s16[520,128]{1,0:T(8,128)(2,1)S(1)}, u32[]{:S(2)}, u32[]{:S(2)}) collective-permute-start(s16[520,128]{1,0:T(8,128)(2,1)S(1)} %get-tuple-element.52), channel_id=1, source_target_pairs={{0,24},{4,28},{8,16},{12,20},{16,8},{20,12},{24,0},{28,4},{1,25},{... | collective-permute-start | bytes 399368 | tf_op jit(solution)/shard_map/ppermute | solution.py:706
  56.4 7.6 %collective-permute-start.3 = (s16[520,128]{1,0:T(8,128)(2,1)S(1)}, s16[520,128]{1,0:T(8,128)(2,1)S(1)}, u32[]{:S(2)}, u32[]{:S(2)}) collective-permute-start(s16[520,128]{1,0:T(8,128)(2,1)S(1)} %get-tuple-element.53), channel_id=1, source_target_pairs={{0,28},{4,24},{8,20},{12,16},{16,12},{20,8},{24,4},{28,0},{1,29},{... | collective-permute-start | bytes 399368 | tf_op jit(solution)/shard_map/ppermute | solution.py:706
  66.1 6.9 %collective-permute-start.16 = (s16[136,128]{1,0:T(8,128)(2,1)S(1)}, s16[136,128]{1,0:T(8,128)(2,1)S(1)}, u32[]{:S(2)}, u32[]{:S(2)}) collective-permute-start(s16[136,128]{1,0:T(8,128)(2,1)S(1)} %get-tuple-element.73.refs_0_), channel_id=1, source_target_pairs={{0,3},{1,0},{2,1},{3,2},{4,7},{5,4},{6,5},{7,6},{8,11},{9,8},{10,9... | collective-permute-start | bytes 104456 | tf_op jit(solution)/shard_map/ppermute | solution.py:709
  77.1 6.5 %collective-permute-start.19 = (s16[1032,128]{1,0:T(8,128)(2,1)S(1)}, s16[1032,128]{1,0:T(8,128)(2,1)S(1)}, u32[]{:S(2)}, u32[]{:S(2)}) collective-permute-start(s16[1032,128]{1,0:T(8,128)(2,1)S(1)} %get-tuple-element.77), channel_id=1, source_target_pairs={{0,16},{4,20},{8,24},{12,28},{16,0},{20,4},{24,8},{28,12},{1,17},{... | collective-permute-start | bytes 792584 | tf_op jit(solution)/shard_map/ppermute | solution.py:706
  78.0 6.9 %collective-permute-start.20 = (s16[1032,128]{1,0:T(8,128)(2,1)S(1)}, s16[1032,128]{1,0:T(8,128)(2,1)S(1)}, u32[]{:S(2)}, u32[]{:S(2)}) collective-permute-start(s16[1032,128]{1,0:T(8,128)(2,1)S(1)} %get-tuple-element.78), channel_id=1, source_target_pairs={{0,8},{4,12},{8,0},{12,4},{16,24},{20,28},{24,16},{28,20},{1,9},{5... | collective-permute-start | bytes 792584 | tf_op jit(solution)/shard_map/ppermute | solution.py:706
  78.8 13.1 %collective-permute-start.21 = (s16[1032,128]{1,0:T(8,128)(2,1)S(1)}, s16[1032,128]{1,0:T(8,128)(2,1)S(1)}, u32[]{:S(2)}, u32[]{:S(2)}) collective-permute-start(s16[1032,128]{1,0:T(8,128)(2,1)S(1)} %get-tuple-element.79), channel_id=1, source_target_pairs={{0,20},{4,16},{8,28},{12,24},{16,4},{20,0},{24,12},{28,8},{1,21},{... | collective-permute-start | bytes 792584 | tf_op jit(solution)/shard_map/ppermute | solution.py:706
  81.5 12.7 %collective-permute-start.22 = (s16[1032,128]{1,0:T(8,128)(2,1)S(1)}, s16[1032,128]{1,0:T(8,128)(2,1)S(1)}, u32[]{:S(2)}, u32[]{:S(2)}) collective-permute-start(s16[1032,128]{1,0:T(8,128)(2,1)S(1)} %get-tuple-element.80), channel_id=1, source_target_pairs={{0,12},{4,8},{8,4},{12,0},{16,28},{20,24},{24,20},{28,16},{1,13},{... | collective-permute-start | bytes 792584 | tf_op jit(solution)/shard_map/ppermute | solution.py:706
  81.5 12.6 %collective-permute-start.23 = (s16[1032,128]{1,0:T(8,128)(2,1)S(1)}, s16[1032,128]{1,0:T(8,128)(2,1)S(1)}, u32[]{:S(2)}, u32[]{:S(2)}) collective-permute-start(s16[1032,128]{1,0:T(8,128)(2,1)S(1)} %get-tuple-element.81), channel_id=1, source_target_pairs={{0,4},{4,0},{8,12},{12,8},{16,20},{20,16},{24,28},{28,24},{1,5},{5... | collective-permute-start | bytes 792584 | tf_op jit(solution)/shard_map/ppermute | solution.py:706
  83.6 14.9 %collective-permute-start.17 = (s16[1032,128]{1,0:T(8,128)(2,1)S(1)}, s16[1032,128]{1,0:T(8,128)(2,1)S(1)}, u32[]{:S(2)}, u32[]{:S(2)}) collective-permute-start(s16[1032,128]{1,0:T(8,128)(2,1)S(1)} %get-tuple-element.74), channel_id=1, source_target_pairs={{0,24},{4,28},{8,16},{12,20},{16,8},{20,12},{24,0},{28,4},{1,25},{... | collective-permute-start | bytes 792584 | tf_op jit(solution)/shard_map/ppermute | solution.py:706
  84.8 18.5 %collective-permute-start.18 = (s16[1032,128]{1,0:T(8,128)(2,1)S(1)}, s16[1032,128]{1,0:T(8,128)(2,1)S(1)}, u32[]{:S(2)}, u32[]{:S(2)}) collective-permute-start(s16[1032,128]{1,0:T(8,128)(2,1)S(1)} %get-tuple-element.75), channel_id=1, source_target_pairs={{0,28},{4,24},{8,20},{12,16},{16,12},{20,8},{24,4},{28,0},{1,29},{... | collective-permute-start | bytes 792584 | tf_op jit(solution)/shard_map/ppermute | solution.py:706
  (12 other events, 293.0 us)
